TPU v7x, 256 devices: a whole 4x4x8 slice. The times are simulated.
256 devices in a mesh: gx: 32 (over x_lo, z, core), gy: 8 (over y, x_hi).
Axes of the slice: x: 4 (x_hi: 2, x_lo: 2; x = x_hi * 2 + x_lo), y: 4, z: 8, core: 2. Of those that a mesh axis runs over, the one named last changes fastest.
Arguments:
- ocean_state: float32 [4, 32, 1024, 1024], P(None, None, 'gx', 'gy'), may hold values from -6 to 6
- barotropic: float32 [3, 1024, 1024], P(None, 'gx', 'gy'), may hold values from -4 to 4
- levels: int32 [1024, 1024], P('gx', 'gy'), may hold values from 0 to 32, as said below
Outputs:
- new_ocean: float32 [4, 32, 1024, 1024], P(None, None, 'gx', 'gy')
- new_barotropic: float32 [3, 1024, 1024], P(None, 'gx', 'gy')
Inputs may be any that keep to these rules, and one draw needn't show every extreme that they name: `levels`: the first and last meridional rows are land (0).
All inputs are finite; a program needn't handle non-finite values.
Results may differ from a plain program's by a relative error of at most 0.00002.
Values sent between devices are 32-bit elements; how exact they have to be, the bound alone decides.
A program may use at most 64 MiB of HBM per device.

v0:
```python
import jax
import jax.numpy as jnp
from jax import lax
from jax.sharding import PartitionSpec as P

K = 32
NSUB = 16


def padded(cells, sides, width):
    for axis, dim in sides:
        count = lax.axis_size(axis)
        head = lax.slice_in_dim(cells, 0, width, axis=dim)
        tail = lax.slice_in_dim(cells, cells.shape[dim] - width, cells.shape[dim], axis=dim)
        cells = jnp.concatenate(
            [
                lax.ppermute(tail, axis, [(i, (i + 1) % count) for i in range(count)]),
                cells,
                lax.ppermute(head, axis, [((i + 1) % count, i) for i in range(count)]),
            ],
            axis=dim,
        )
    return cells


def slices(a):
    return (
        a[..., 1:-1, 1:-1],
        a[..., 2:, 1:-1],
        a[..., :-2, 1:-1],
        a[..., 1:-1, 2:],
        a[..., 1:-1, :-2],
    )


def shrink(a):
    return a[..., 1:-1, 1:-1]


def baroclinic(ext, fcor, near_fn):
    u_all, v_all, t_all, s_all, m_all = (ext[0], ext[1], ext[2], ext[3], ext[4])
    press = jnp.cumsum(m_all * (0.1 * s_all - 0.2 * t_all), axis=0)
    mc, me, mw, mn, ms = near_fn(m_all)

    def lapl(q):
        qc, qe, qw, qn, qs = near_fn(q)
        return mc * me * (qe - qc) + mc * mw * (qw - qc) + mc * mn * (qn - qc) + mc * ms * (qs - qc)

    def diffx(q):
        qc, qe, qw, qn, qs = near_fn(q)
        return 0.5 * (mc * me * (qe - qc) + mc * mw * (qc - qw))

    def diffy(q):
        qc, qe, qw, qn, qs = near_fn(q)
        return 0.5 * (mc * mn * (qn - qc) + mc * ms * (qc - qs))

    uc = near_fn(u_all)[0]
    vc = near_fn(v_all)[0]
    tc = near_fn(t_all)[0]
    sc = near_fn(s_all)[0]
    tend_u = lapl(u_all) + fcor * vc - diffx(press)
    tend_v = lapl(v_all) - fcor * uc - diffy(press)
    new_t = mc * (tc + 0.1 * (lapl(t_all) - uc * diffx(t_all) - vc * diffy(t_all)))
    new_s = mc * (sc + 0.1 * (lapl(s_all) - uc * diffx(s_all) - vc * diffy(s_all)))
    return (uc + 0.1 * tend_u, vc + 0.1 * tend_v, new_t, new_s, tend_u, tend_v, mc)


def substep(eta, vel_u, vel_v, depth, force_u, force_v, fcor, near_fn, crop):
    wet = (depth > 0).astype(depth.dtype)
    hc, he, hw, hn, hs = near_fn(depth)
    wc, we, ww, wn, ws = near_fn(wet)
    uc, ue, uw, un, us = near_fn(vel_u)
    vc, ve, vw, vn, vs = near_fn(vel_v)
    flux_e = 0.5 * (hc * uc + he * ue) * wc * we
    flux_w = 0.5 * (hw * uw + hc * uc) * wc * ww
    flux_n = 0.5 * (hc * vc + hn * vn) * wc * wn
    flux_s = 0.5 * (hs * vs + hc * vc) * wc * ws
    eta_mid = wc * (crop(eta) - 0.3 * (flux_e - flux_w + (flux_n - flux_s)))
    wet_mid = crop(wet)
    ec, ee, ew, en, es = near_fn(eta_mid)
    mc, me, mw, mn, ms = near_fn(wet_mid)
    grad_x = 0.5 * (mc * me * (ee - ec) + mc * mw * (ec - ew))
    grad_y = 0.5 * (mc * mn * (en - ec) + mc * ms * (ec - es))
    old_u = crop(crop(vel_u))
    old_v = crop(crop(vel_v))
    fc = crop(crop(fcor))
    new_u = mc * (old_u + 0.3 * (-grad_x + fc * old_v + crop(crop(force_u))))
    new_v = mc * (old_v + 0.3 * (-grad_y - fc * old_u + crop(crop(force_v))))
    return (crop(eta_mid), new_u, new_v)


def subcycles(
    state, statics, extend_statics, extend_state, row_start, row_total, margin, per_block
):
    width_x = state.shape[1]
    width_y = state.shape[2]
    ext_static = extend_statics(statics)
    rows_idx = (row_start - margin + jnp.arange(width_y + 2 * margin)) % row_total
    fline = 0.5 * (2.0 * (rows_idx.astype(jnp.float32) + 0.5) / row_total - 1.0)
    fcor_ext = jnp.broadcast_to(fline[None, :], (width_x + 2 * margin, width_y + 2 * margin))

    def block(index, carry):
        current, total = carry
        ext = extend_state(current)
        eta, vel_u, vel_v = (ext[0], ext[1], ext[2])
        depth, force_u, force_v = (ext_static[0], ext_static[1], ext_static[2])
        eta, vel_u, vel_v = substep(
            eta, vel_u, vel_v, depth, force_u, force_v, fcor_ext, slices, shrink
        )
        total = total + jnp.stack([vel_u, vel_v])
        return (jnp.stack([eta, vel_u, vel_v]), total)

    zeros = jnp.zeros((2, width_x, width_y), jnp.float32)
    final, total = lax.fori_loop(0, NSUB // per_block, block, (state, zeros))
    return jnp.concatenate([final, total * (1.0 / NSUB)], axis=0)


def per_device(ocean_state, barotropic, levels):
    tile_x = levels.shape[0]
    tile_y = levels.shape[1]
    ks = jnp.arange(K)
    lev = levels.astype(jnp.float32)
    flat = jnp.concatenate([ocean_state.reshape(4 * K, tile_x, tile_y), lev[None]], axis=0)
    widened = padded(flat, (("gx", 1), ("gy", 2)), 1)
    fields = widened[: 4 * K].reshape(4, K, tile_x + 2, tile_y + 2)
    lev_ext = widened[4 * K]
    wet_ext = (ks.astype(jnp.float32)[:, None, None] < lev_ext[None, :, :]).astype(jnp.float32)
    ext = jnp.concatenate([fields, wet_ext[None]], axis=0)
    row_start = lax.axis_index("gy") * tile_y
    row_total = tile_y * lax.axis_size("gy")
    yy = (row_start + jnp.arange(tile_y)).astype(jnp.float32)
    fline = 0.5 * (2.0 * (yy + 0.5) / row_total - 1.0)
    ustar, vstar, new_t, new_s, tend_u, tend_v, mc = baroclinic(ext, fline, slices)
    inverse = 1.0 / jnp.maximum(lev, 1.0)
    force_u = jnp.sum(mc * tend_u, axis=0) * inverse
    force_v = jnp.sum(mc * tend_v, axis=0) * inverse
    depth = lev / K
    per_block = 1
    margin = 2 * per_block
    packed = jnp.concatenate([barotropic, jnp.stack([depth, force_u, force_v])], axis=0)
    strip = lax.all_to_all(packed, "gy", split_axis=1, concat_axis=2, tiled=True)

    def pad_rows(a):
        return jnp.pad(a, ((0, 0), (0, 0), (margin, margin)))

    def strip_statics(a):
        return pad_rows(padded(a, ((("gx", "gy"), 1),), margin))

    def strip_state(a):
        return pad_rows(padded(a, ((("gx", "gy"), 1),), margin))

    result = subcycles(
        strip[0:3], strip[3:6], strip_statics, strip_state, 0, row_total, margin, per_block
    )
    result = lax.all_to_all(result, "gy", split_axis=2, concat_axis=1, tiled=True)
    col_u = jnp.sum(mc * ustar, axis=0) * inverse
    col_v = jnp.sum(mc * vstar, axis=0) * inverse
    new_u = mc * (ustar - col_u + result[3])
    new_v = mc * (vstar - col_v + result[4])
    return (jnp.stack([new_u, new_v, new_t, new_s]), result[0:3])


def solution(mesh):
    in_specs = (P(None, None, "gx", "gy"), P(None, "gx", "gy"), P("gx", "gy"))
    out_specs = (P(None, None, "gx", "gy"), P(None, "gx", "gy"))
    return jax.shard_map(
        per_device, mesh=mesh, in_specs=in_specs, out_specs=out_specs, check_vma=False
    )
```

profile of v0, /device:TPU:8, one launch (start us, length us, event | category | flops | bytes accessed | tf_op | source)
XLA Modules:
  0.0 354.2 jit_solution(6598972396860938404)
XLA Ops:
  2.8 6.3 %collective-permute-start.3 = (f32[129,1,128]{2,1,0:T(1,128)S(1)}, f32[129,1,128]{2,1,0:T(1,128)S(1)}, u32[]{:S(2)}, u32[]{:S(2)}) collective-permute-start(f32[129,1,128]{2,1,0:T(1,128)S(1)} %get-tuple-element.140), channel_id=1, source_target_pairs={{8,0},{16,8},{24,16},{32,24},{40,32},{48,40},{56,48},{64,56},{72,6... | collective-permute-start | bytes 198152 | tf_op jit(solution)/shard_map/ppermute | solution.py:19
  11.0 3.9 %collective-permute-done.2 = f32[129,1,128]{2,1,0:T(1,128)S(1)} collective-permute-done((f32[129,1,128]{2,1,0:T(1,128)S(1)}, f32[129,1,128]{2,1,0:T(1,128)S(1)}, u32[]{:S(2)}, u32[]{:S(2)}) %collective-permute-start.2) | collective-permute-done | bytes 66080 | tf_op jit(solution)/shard_map/ppermute | solution.py:17
  15.3 3.2 fusion.144
  18.5 3.1 copy.26
  24.3 3.1 copy.25
  29.0 3.0 copy.28
  33.7 3.1 copy.27
  41.7 5.2 %multiply_reduce_fusion.3 = (f32[32,128]{1,0:T(8,128)S(1)}, f32[32,128]{1,0:T(8,128)S(1)}, f32[32,128]{1,0:T(8,128)S(1)}, f32[32,128]{1,0:T(8,128)S(1)}, f32[32,...) fusion(f32[32,34,130]{2,1,0:T(8,128)S(1)} %compare_convert_fusi, ...), kind=kLoop, calls=%fused_computation.218 | loop fusion | flops 10469376 | bytes 11783952 | tf_op jit(solution)/shard_map/reduce_sum | solution.py:156
  48.3 8.1 %all-to-all-start = ((f32[6,32,128]{2,0,1:T(8,128)}), f32[6,32,128]{2,0,1:T(8,128)}, u32[]{:S(2)}, u32[]{:S(2)}) async-start(f32[6,32,128]{2,0,1:T(8,128)} %pad_maximum_fusion.26), calls=%async_computation | async-start | bytes 262144 | tf_op jit(solution)/shard_map/all_to_all | solution.py:141
  56.4 6.7 %all-to-all-done = f32[6,32,128]{2,0,1:T(8,128)} async-done(((f32[6,32,128]{2,0,1:T(8,128)}), f32[6,32,128]{2,0,1:T(8,128)}, u32[]{:S(2)}, u32[]{:S(2)}) %all-to-all-start) | async-done | bytes 98336 | tf_op jit(solution)/shard_map/all_to_all | solution.py:141
  71.8 3.7 %multiply_bitcast_fusion = f32[1,32,32,128]{3,2,1,0:T(8,128)} fusion(f32[32,32,128]{2,1,0:T(8,128)} %get-tuple-element.124, f32[32,32,128]{2,1,0:T(8,128)} %get-tuple-element.123, f32[129,1,128]{2,1,0:T(1,128)S(1)} %collective-permute-done.3, f32[1,32,128]{2,1,0:T(8,128)} %copy-done.9, f32[128,32,128]{2,1,0:T(8,128)S(1)} %bitcast.217, ...), kind=kLoop, calls=%fused_computation.211 | loop fusion | flops 4980736 | bytes 6999312 | tf_op jit(solution)/shard_map/stack | solution.py:160
  78.9 230.8 %while.16 = (s32[]{:T(128)}, f32[3,4,1024]{2,1,0:T(4,128)S(1)}, f32[2,4,1024]{2,1,0:T(4,128)}, f32[3,8,1028]{2,1,0:T(8,128)}, f32[8,1028]{1,0:T(8,128)}, /*index=5*/s32[]{:T(128)}, s32[]{:T(128)}) while((s32[]{:T(128)}, f32[3,4,1024]{2,1,0:T(4,128)S(1)}, f32[2,4,1024]{2,1,0:T(4,128)}, f32[3,8,1028]{2,1,0:T(8,128)}, ...), condition=%wide.region_5.6_spmd.clone.clone, body=%wide.region_4.5_spmd.clone.clone.sunk | while | flops 558227 | bytes 1969295 | solution.py:114
  85.3 2.7 collective-permute-done.1
  98.0 4.4 %collective-permute-done.1 = f32[3,2,1024]{2,1,0:T(2,128)} collective-permute-done((f32[3,2,1024]{2,1,0:T(2,128)}, f32[3,2,1024]{2,1,0:T(2,128)}, u32[]{:S(2)}, u32[]{:S(2)}) %collective-permute-start.1) | collective-permute-done | bytes 24608 | tf_op jit(solution)/shard_map/while/body/eval_jaxpr/ppermute | solution.py:17
  107.5 3.3 collective-permute-start
  113.2 4.1 %collective-permute-done.1 = f32[3,2,1024]{2,1,0:T(2,128)} collective-permute-done((f32[3,2,1024]{2,1,0:T(2,128)}, f32[3,2,1024]{2,1,0:T(2,128)}, u32[]{:S(2)}, u32[]{:S(2)}) %collective-permute-start.1) | collective-permute-done | bytes 24608 | tf_op jit(solution)/shard_map/while/body/eval_jaxpr/ppermute | solution.py:17
  122.4 2.9 collective-permute-start
  128.1 3.7 %collective-permute-done.1 = f32[3,2,1024]{2,1,0:T(2,128)} collective-permute-done((f32[3,2,1024]{2,1,0:T(2,128)}, f32[3,2,1024]{2,1,0:T(2,128)}, u32[]{:S(2)}, u32[]{:S(2)}) %collective-permute-start.1) | collective-permute-done | bytes 24608 | tf_op jit(solution)/shard_map/while/body/eval_jaxpr/ppermute | solution.py:17
  136.8 2.9 collective-permute-start
  142.6 3.7 %collective-permute-done.1 = f32[3,2,1024]{2,1,0:T(2,128)} collective-permute-done((f32[3,2,1024]{2,1,0:T(2,128)}, f32[3,2,1024]{2,1,0:T(2,128)}, u32[]{:S(2)}, u32[]{:S(2)}) %collective-permute-start.1) | collective-permute-done | bytes 24608 | tf_op jit(solution)/shard_map/while/body/eval_jaxpr/ppermute | solution.py:17
  151.3 2.9 collective-permute-start
  157.0 3.7 %collective-permute-done.1 = f32[3,2,1024]{2,1,0:T(2,128)} collective-permute-done((f32[3,2,1024]{2,1,0:T(2,128)}, f32[3,2,1024]{2,1,0:T(2,128)}, u32[]{:S(2)}, u32[]{:S(2)}) %collective-permute-start.1) | collective-permute-done | bytes 24608 | tf_op jit(solution)/shard_map/while/body/eval_jaxpr/ppermute | solution.py:17
  165.7 2.9 collective-permute-start
  171.5 3.7 %collective-permute-done.1 = f32[3,2,1024]{2,1,0:T(2,128)} collective-permute-done((f32[3,2,1024]{2,1,0:T(2,128)}, f32[3,2,1024]{2,1,0:T(2,128)}, u32[]{:S(2)}, u32[]{:S(2)}) %collective-permute-start.1) | collective-permute-done | bytes 24608 | tf_op jit(solution)/shard_map/while/body/eval_jaxpr/ppermute | solution.py:17
  180.2 2.9 collective-permute-start
  185.9 3.7 %collective-permute-done.1 = f32[3,2,1024]{2,1,0:T(2,128)} collective-permute-done((f32[3,2,1024]{2,1,0:T(2,128)}, f32[3,2,1024]{2,1,0:T(2,128)}, u32[]{:S(2)}, u32[]{:S(2)}) %collective-permute-start.1) | collective-permute-done | bytes 24608 | tf_op jit(solution)/shard_map/while/body/eval_jaxpr/ppermute | solution.py:17
  194.7 2.9 collective-permute-start
  200.4 3.7 %collective-permute-done.1 = f32[3,2,1024]{2,1,0:T(2,128)} collective-permute-done((f32[3,2,1024]{2,1,0:T(2,128)}, f32[3,2,1024]{2,1,0:T(2,128)}, u32[]{:S(2)}, u32[]{:S(2)}) %collective-permute-start.1) | collective-permute-done | bytes 24608 | tf_op jit(solution)/shard_map/while/body/eval_jaxpr/ppermute | solution.py:17
  209.1 2.9 collective-permute-start
  214.9 3.7 %collective-permute-done.1 = f32[3,2,1024]{2,1,0:T(2,128)} collective-permute-done((f32[3,2,1024]{2,1,0:T(2,128)}, f32[3,2,1024]{2,1,0:T(2,128)}, u32[]{:S(2)}, u32[]{:S(2)}) %collective-permute-start.1) | collective-permute-done | bytes 24608 | tf_op jit(solution)/shard_map/while/body/eval_jaxpr/ppermute | solution.py:17
  223.6 2.9 collective-permute-start
  229.3 3.7 %collective-permute-done.1 = f32[3,2,1024]{2,1,0:T(2,128)} collective-permute-done((f32[3,2,1024]{2,1,0:T(2,128)}, f32[3,2,1024]{2,1,0:T(2,128)}, u32[]{:S(2)}, u32[]{:S(2)}) %collective-permute-start.1) | collective-permute-done | bytes 24608 | tf_op jit(solution)/shard_map/while/body/eval_jaxpr/ppermute | solution.py:17
  238.0 2.9 collective-permute-start
  243.8 3.7 %collective-permute-done.1 = f32[3,2,1024]{2,1,0:T(2,128)} collective-permute-done((f32[3,2,1024]{2,1,0:T(2,128)}, f32[3,2,1024]{2,1,0:T(2,128)}, u32[]{:S(2)}, u32[]{:S(2)}) %collective-permute-start.1) | collective-permute-done | bytes 24608 | tf_op jit(solution)/shard_map/while/body/eval_jaxpr/ppermute | solution.py:17
  252.5 2.9 collective-permute-start
  258.2 3.7 %collective-permute-done.1 = f32[3,2,1024]{2,1,0:T(2,128)} collective-permute-done((f32[3,2,1024]{2,1,0:T(2,128)}, f32[3,2,1024]{2,1,0:T(2,128)}, u32[]{:S(2)}, u32[]{:S(2)}) %collective-permute-start.1) | collective-permute-done | bytes 24608 | tf_op jit(solution)/shard_map/while/body/eval_jaxpr/ppermute | solution.py:17
  267.0 2.9 collective-permute-start
  272.7 3.7 %collective-permute-done.1 = f32[3,2,1024]{2,1,0:T(2,128)} collective-permute-done((f32[3,2,1024]{2,1,0:T(2,128)}, f32[3,2,1024]{2,1,0:T(2,128)}, u32[]{:S(2)}, u32[]{:S(2)}) %collective-permute-start.1) | collective-permute-done | bytes 24608 | tf_op jit(solution)/shard_map/while/body/eval_jaxpr/ppermute | solution.py:17
  281.4 2.9 collective-permute-start
  287.2 3.7 %collective-permute-done.1 = f32[3,2,1024]{2,1,0:T(2,128)} collective-permute-done((f32[3,2,1024]{2,1,0:T(2,128)}, f32[3,2,1024]{2,1,0:T(2,128)}, u32[]{:S(2)}, u32[]{:S(2)}) %collective-permute-start.1) | collective-permute-done | bytes 24608 | tf_op jit(solution)/shard_map/while/body/eval_jaxpr/ppermute | solution.py:17
  295.9 2.9 collective-permute-start
  301.6 3.7 %collective-permute-done.1 = f32[3,2,1024]{2,1,0:T(2,128)} collective-permute-done((f32[3,2,1024]{2,1,0:T(2,128)}, f32[3,2,1024]{2,1,0:T(2,128)}, u32[]{:S(2)}, u32[]{:S(2)}) %collective-permute-start.1) | collective-permute-done | bytes 24608 | tf_op jit(solution)/shard_map/while/body/eval_jaxpr/ppermute | solution.py:17
  313.6 4.4 %reshape.63 = f32[8,1,2560]{2,1,0:T(1,128)} reshape(f32[1024,4,5]{2,1,0:T(4,128)} %bitcast.221) | data formatting | bytes 163840
  318.0 7.5 %all-to-all-start.1 = ((f32[8,1,2560]{2,1,0:T(1,128)}), f32[8,1,2560]{2,1,0:T(1,128)}, u32[]{:S(2)}, u32[]{:S(2)}) async-start(f32[8,1,2560]{2,1,0:T(1,128)} %reshape.63), calls=%async_computation.1 | async-start | bytes 163840 | tf_op jit(solution)/shard_map/all_to_all | solution.py:155
  325.5 3.6 %multiply_bitcast_fusion.1 = f32[1,32,32,128]{3,2,1,0:T(8,128)} fusion(f32[32,32,128]{2,1,0:T(8,128)} %get-tuple-element.124, f32[32,32,128]{2,1,0:T(8,128)} %get-tuple-element.123, f32[129,1,128]{2,1,0:T(1,128)S(1)} %copy-done.4, f32[1,32,128]{2,1,0:T(8,128)} %copy-done.9, f32[128,32,128]{2,1,0:T(8,128)S(1)} %bitcast.218, f32[129,1,128]{2,1,0:T(1,128)S(1)} %copy-done.6, ...), kind=kLoop, calls=%fused_computation.212 | loop fusion | flops 4980736 | bytes 6999312 | tf_op jit(solution)/shard_map/stack | solution.py:160
  329.2 2.9 all-to-all-done.1
  334.4 3.9 %reshape.64 = f32[1024,4,5]{2,1,0:T(4,128)} reshape(f32[8,2560]{1,0:T(8,128)S(1)} %reduce) | data formatting | bytes 163840
  338.3 6.4 %fusion.145 = (f32[1,8,4,128]{0,2,3,1:T(4,128)}, f32[1,8,4,128]{0,2,3,1:T(4,128)}) fusion(f32[5,8,4,128]{0,2,3,1:T(4,128)} %bitcast.219), kind=kLoop, calls=%fused_computation.257 | loop fusion | bytes 65536 | tf_op jit(solution)/shard_map/slice | solution.py:158
  (269 shorter events, 175.4 us)
Async XLA Ops:
  0.6 14.3 %copy-start = (f32[4,32,32,128]{3,2,1,0:T(8,128)S(1)}, f32[4,32,32,128]{3,2,1,0:T(8,128)}, u32[]{:S(2)}) copy-start(f32[4,32,32,128]{3,2,1,0:T(8,128)} %param.5) | copy-start | bytes 6291460
  1.5 35.3 %copy-start.9 = (f32[1,32,128]{2,1,0:T(8,128)}, f32[1,32,128]{2,1,0:T(8,128)S(1)}, u32[]{:S(2)}) copy-start(f32[1,32,128]{2,1,0:T(8,128)S(1)} %convert_bitcast_fusion) | copy-start | bytes 49156
  2.8 8.2 %collective-permute-start.3 = (f32[129,1,128]{2,1,0:T(1,128)S(1)}, f32[129,1,128]{2,1,0:T(1,128)S(1)}, u32[]{:S(2)}, u32[]{:S(2)}) collective-permute-start(f32[129,1,128]{2,1,0:T(1,128)S(1)} %get-tuple-element.140), channel_id=1, source_target_pairs={{8,0},{16,8},{24,16},{32,24},{40,32},{48,40},{56,48},{64,56},{72,6... | collective-permute-start | bytes 198152 | tf_op jit(solution)/shard_map/ppermute | solution.py:19
  9.1 5.8 %collective-permute-start.2 = (f32[129,1,128]{2,1,0:T(1,128)S(1)}, f32[129,1,128]{2,1,0:T(1,128)S(1)}, u32[]{:S(2)}, u32[]{:S(2)}) collective-permute-start(f32[129,1,128]{2,1,0:T(1,128)S(1)} %get-tuple-element.139), channel_id=1, source_target_pairs={{0,8},{8,16},{16,24},{24,32},{32,40},{40,48},{48,56},{56,64},{64,7... | collective-permute-start | bytes 198152 | tf_op jit(solution)/shard_map/ppermute | solution.py:17
  11.0 60.8 %copy-start.3 = (f32[129,1,128]{2,1,0:T(1,128)}, f32[129,1,128]{2,1,0:T(1,128)S(1)}, u32[]{:S(2)}) copy-start(f32[129,1,128]{2,1,0:T(1,128)S(1)} %collective-permute-done.3) | copy-start | bytes 198148
  14.9 56.9 %copy-start.5 = (f32[129,1,128]{2,1,0:T(1,128)}, f32[129,1,128]{2,1,0:T(1,128)S(1)}, u32[]{:S(2)}) copy-start(f32[129,1,128]{2,1,0:T(1,128)S(1)} %collective-permute-done.2) | copy-start | bytes 198148
  18.5 9.8 %copy-start.16 = (f32[3,32,128]{2,1,0:T(8,128)S(1)}, f32[3,32,128]{2,1,0:T(8,128)}, u32[]{:S(2)}) copy-start(f32[3,32,128]{2,1,0:T(8,128)} %param.6) | copy-start | bytes 147460
  21.6 7.4 %collective-permute-start.5 = (f32[129,34,1]{0,2,1:T(1,128)S(1)}, f32[129,34,1]{0,2,1:T(1,128)S(1)}, u32[]{:S(2)}, u32[]{:S(2)}) collective-permute-start(f32[129,34,1]{0,2,1:T(1,128)S(1)} %copy.26), channel_id=1, source_target_pairs={{1,0},{2,1},{3,2},{4,3},{5,4},{6,5},{7,6},{0,7},{9,8},{10,9},{11,1... | collective-permute-start | bytes 52640 | tf_op jit(solution)/shard_map/ppermute | solution.py:19
  27.4 6.4 %collective-permute-start.4 = (f32[129,34,1]{0,2,1:T(1,128)S(1)}, f32[129,34,1]{0,2,1:T(1,128)S(1)}, u32[]{:S(2)}, u32[]{:S(2)}) collective-permute-start(f32[129,34,1]{0,2,1:T(1,128)S(1)} %copy.25), channel_id=1, source_target_pairs={{0,1},{1,2},{2,3},{3,4},{4,5},{5,6},{6,7},{7,0},{8,9},{9,10},{10,1... | collective-permute-start | bytes 52640 | tf_op jit(solution)/shard_map/ppermute | solution.py:17
  41.7 5.9 %copy-start.11 = (f32[3,32,128]{2,0,1:T(4,128)S(1)}, f32[3,32,128]{2,0,1:T(4,128)}, u32[]{:S(2)}) copy-start(f32[3,32,128]{2,0,1:T(4,128)} %copy.31) | copy-start | bytes 147460
  48.3 14.8 %all-to-all-start = ((f32[6,32,128]{2,0,1:T(8,128)}), f32[6,32,128]{2,0,1:T(8,128)}, u32[]{:S(2)}, u32[]{:S(2)}) async-start(f32[6,32,128]{2,0,1:T(8,128)} %pad_maximum_fusion.26), calls=%async_computation | async-start | bytes 262144 | tf_op jit(solution)/shard_map/all_to_all | solution.py:141
  68.3 7.3 %collective-permute-start.7 = (f32[3,2,1024]{2,1,0:T(2,128)}, f32[3,2,1024]{2,1,0:T(2,128)}, u32[]{:S(2)}, u32[]{:S(2)}) collective-permute-start(f32[3,2,1024]{2,1,0:T(2,128)} %get-tuple-element.146), channel_id=1, source_target_pairs={{1,0},{2,1},{3,2},{4,3},{5,4},{6,5},{7,6},{8,7},{9,8},{10,9},{11,1... | collective-permute-start | bytes 73736 | tf_op jit(solution)/shard_map/ppermute | solution.py:19
  70.1 6.5 %collective-permute-start.6 = (f32[3,2,1024]{2,1,0:T(2,128)}, f32[3,2,1024]{2,1,0:T(2,128)}, u32[]{:S(2)}, u32[]{:S(2)}) collective-permute-start(f32[3,2,1024]{2,1,0:T(2,128)} %get-tuple-element.145), channel_id=1, source_target_pairs={{0,1},{1,2},{2,3},{3,4},{4,5},{5,6},{6,7},{7,8},{8,9},{9,10},{10,1... | collective-permute-start | bytes 73736 | tf_op jit(solution)/shard_map/ppermute | solution.py:17
  79.5 5.7 %collective-permute-start = (f32[3,2,1024]{2,1,0:T(2,128)}, f32[3,2,1024]{2,1,0:T(2,128)S(1)}, u32[]{:S(2)}, u32[]{:S(2)}) collective-permute-start(f32[3,2,1024]{2,1,0:T(2,128)} %get-tuple-element.194), channel_id=1, source_target_pairs={{1,0},{2,1},{3,2},{4,3},{5,4},{6,5},{7,6},{8,7},{9,8},{10,9},{11,1... | collective-permute-start | bytes 73736 | tf_op jit(solution)/shard_map/while/body/eval_jaxpr/ppermute | solution.py:19
  81.4 6.5 %collective-permute-start.1 = (f32[3,2,1024]{2,1,0:T(2,128)}, f32[3,2,1024]{2,1,0:T(2,128)}, u32[]{:S(2)}, u32[]{:S(2)}) collective-permute-start(f32[3,2,1024]{2,1,0:T(2,128)} %get-tuple-element.195), channel_id=1, source_target_pairs={{0,1},{1,2},{2,3},{3,4},{4,5},{5,6},{6,7},{7,8},{8,9},{9,10},{10,1... | collective-permute-start | bytes 73736 | tf_op jit(solution)/shard_map/while/body/eval_jaxpr/ppermute | solution.py:17
  92.2 5.7 %collective-permute-start = (f32[3,2,1024]{2,1,0:T(2,128)}, f32[3,2,1024]{2,1,0:T(2,128)S(1)}, u32[]{:S(2)}, u32[]{:S(2)}) collective-permute-start(f32[3,2,1024]{2,1,0:T(2,128)} %get-tuple-element.194), channel_id=1, source_target_pairs={{1,0},{2,1},{3,2},{4,3},{5,4},{6,5},{7,6},{8,7},{9,8},{10,9},{11,1... | collective-permute-start | bytes 73736 | tf_op jit(solution)/shard_map/while/body/eval_jaxpr/ppermute | solution.py:19
  94.8 7.6 %collective-permute-start.1 = (f32[3,2,1024]{2,1,0:T(2,128)}, f32[3,2,1024]{2,1,0:T(2,128)}, u32[]{:S(2)}, u32[]{:S(2)}) collective-permute-start(f32[3,2,1024]{2,1,0:T(2,128)} %get-tuple-element.195), channel_id=1, source_target_pairs={{0,1},{1,2},{2,3},{3,4},{4,5},{5,6},{6,7},{7,8},{8,9},{9,10},{10,1... | collective-permute-start | bytes 73736 | tf_op jit(solution)/shard_map/while/body/eval_jaxpr/ppermute | solution.py:17
  107.5 5.7 %collective-permute-start = (f32[3,2,1024]{2,1,0:T(2,128)}, f32[3,2,1024]{2,1,0:T(2,128)S(1)}, u32[]{:S(2)}, u32[]{:S(2)}) collective-permute-start(f32[3,2,1024]{2,1,0:T(2,128)} %get-tuple-element.194), channel_id=1, source_target_pairs={{1,0},{2,1},{3,2},{4,3},{5,4},{6,5},{7,6},{8,7},{9,8},{10,9},{11,1... | collective-permute-start | bytes 73736 | tf_op jit(solution)/shard_map/while/body/eval_jaxpr/ppermute | solution.py:19
  110.7 6.5 %collective-permute-start.1 = (f32[3,2,1024]{2,1,0:T(2,128)}, f32[3,2,1024]{2,1,0:T(2,128)}, u32[]{:S(2)}, u32[]{:S(2)}) collective-permute-start(f32[3,2,1024]{2,1,0:T(2,128)} %get-tuple-element.195), channel_id=1, source_target_pairs={{0,1},{1,2},{2,3},{3,4},{4,5},{5,6},{6,7},{7,8},{8,9},{9,10},{10,1... | collective-permute-start | bytes 73736 | tf_op jit(solution)/shard_map/while/body/eval_jaxpr/ppermute | solution.py:17
  122.4 5.7 %collective-permute-start = (f32[3,2,1024]{2,1,0:T(2,128)}, f32[3,2,1024]{2,1,0:T(2,128)S(1)}, u32[]{:S(2)}, u32[]{:S(2)}) collective-permute-start(f32[3,2,1024]{2,1,0:T(2,128)} %get-tuple-element.194), channel_id=1, source_target_pairs={{1,0},{2,1},{3,2},{4,3},{5,4},{6,5},{7,6},{8,7},{9,8},{10,9},{11,1... | collective-permute-start | bytes 73736 | tf_op jit(solution)/shard_map/while/body/eval_jaxpr/ppermute | solution.py:19
  125.2 6.5 %collective-permute-start.1 = (f32[3,2,1024]{2,1,0:T(2,128)}, f32[3,2,1024]{2,1,0:T(2,128)}, u32[]{:S(2)}, u32[]{:S(2)}) collective-permute-start(f32[3,2,1024]{2,1,0:T(2,128)} %get-tuple-element.195), channel_id=1, source_target_pairs={{0,1},{1,2},{2,3},{3,4},{4,5},{5,6},{6,7},{7,8},{8,9},{9,10},{10,1... | collective-permute-start | bytes 73736 | tf_op jit(solution)/shard_map/while/body/eval_jaxpr/ppermute | solution.py:17
  136.8 5.7 %collective-permute-start = (f32[3,2,1024]{2,1,0:T(2,128)}, f32[3,2,1024]{2,1,0:T(2,128)S(1)}, u32[]{:S(2)}, u32[]{:S(2)}) collective-permute-start(f32[3,2,1024]{2,1,0:T(2,128)} %get-tuple-element.194), channel_id=1, source_target_pairs={{1,0},{2,1},{3,2},{4,3},{5,4},{6,5},{7,6},{8,7},{9,8},{10,9},{11,1... | collective-permute-start | bytes 73736 | tf_op jit(solution)/shard_map/while/body/eval_jaxpr/ppermute | solution.py:19
  139.7 6.5 %collective-permute-start.1 = (f32[3,2,1024]{2,1,0:T(2,128)}, f32[3,2,1024]{2,1,0:T(2,128)}, u32[]{:S(2)}, u32[]{:S(2)}) collective-permute-start(f32[3,2,1024]{2,1,0:T(2,128)} %get-tuple-element.195), channel_id=1, source_target_pairs={{0,1},{1,2},{2,3},{3,4},{4,5},{5,6},{6,7},{7,8},{8,9},{9,10},{10,1... | collective-permute-start | bytes 73736 | tf_op jit(solution)/shard_map/while/body/eval_jaxpr/ppermute | solution.py:17
  151.3 5.7 %collective-permute-start = (f32[3,2,1024]{2,1,0:T(2,128)}, f32[3,2,1024]{2,1,0:T(2,128)S(1)}, u32[]{:S(2)}, u32[]{:S(2)}) collective-permute-start(f32[3,2,1024]{2,1,0:T(2,128)} %get-tuple-element.194), channel_id=1, source_target_pairs={{1,0},{2,1},{3,2},{4,3},{5,4},{6,5},{7,6},{8,7},{9,8},{10,9},{11,1... | collective-permute-start | bytes 73736 | tf_op jit(solution)/shard_map/while/body/eval_jaxpr/ppermute | solution.py:19
  154.1 6.5 %collective-permute-start.1 = (f32[3,2,1024]{2,1,0:T(2,128)}, f32[3,2,1024]{2,1,0:T(2,128)}, u32[]{:S(2)}, u32[]{:S(2)}) collective-permute-start(f32[3,2,1024]{2,1,0:T(2,128)} %get-tuple-element.195), channel_id=1, source_target_pairs={{0,1},{1,2},{2,3},{3,4},{4,5},{5,6},{6,7},{7,8},{8,9},{9,10},{10,1... | collective-permute-start | bytes 73736 | tf_op jit(solution)/shard_map/while/body/eval_jaxpr/ppermute | solution.py:17
  165.7 5.7 %collective-permute-start = (f32[3,2,1024]{2,1,0:T(2,128)}, f32[3,2,1024]{2,1,0:T(2,128)S(1)}, u32[]{:S(2)}, u32[]{:S(2)}) collective-permute-start(f32[3,2,1024]{2,1,0:T(2,128)} %get-tuple-element.194), channel_id=1, source_target_pairs={{1,0},{2,1},{3,2},{4,3},{5,4},{6,5},{7,6},{8,7},{9,8},{10,9},{11,1... | collective-permute-start | bytes 73736 | tf_op jit(solution)/shard_map/while/body/eval_jaxpr/ppermute | solution.py:19
  168.6 6.5 %collective-permute-start.1 = (f32[3,2,1024]{2,1,0:T(2,128)}, f32[3,2,1024]{2,1,0:T(2,128)}, u32[]{:S(2)}, u32[]{:S(2)}) collective-permute-start(f32[3,2,1024]{2,1,0:T(2,128)} %get-tuple-element.195), channel_id=1, source_target_pairs={{0,1},{1,2},{2,3},{3,4},{4,5},{5,6},{6,7},{7,8},{8,9},{9,10},{10,1... | collective-permute-start | bytes 73736 | tf_op jit(solution)/shard_map/while/body/eval_jaxpr/ppermute | solution.py:17
  180.2 5.7 %collective-permute-start = (f32[3,2,1024]{2,1,0:T(2,128)}, f32[3,2,1024]{2,1,0:T(2,128)S(1)}, u32[]{:S(2)}, u32[]{:S(2)}) collective-permute-start(f32[3,2,1024]{2,1,0:T(2,128)} %get-tuple-element.194), channel_id=1, source_target_pairs={{1,0},{2,1},{3,2},{4,3},{5,4},{6,5},{7,6},{8,7},{9,8},{10,9},{11,1... | collective-permute-start | bytes 73736 | tf_op jit(solution)/shard_map/while/body/eval_jaxpr/ppermute | solution.py:19
  183.0 6.5 %collective-permute-start.1 = (f32[3,2,1024]{2,1,0:T(2,128)}, f32[3,2,1024]{2,1,0:T(2,128)}, u32[]{:S(2)}, u32[]{:S(2)}) collective-permute-start(f32[3,2,1024]{2,1,0:T(2,128)} %get-tuple-element.195), channel_id=1, source_target_pairs={{0,1},{1,2},{2,3},{3,4},{4,5},{5,6},{6,7},{7,8},{8,9},{9,10},{10,1... | collective-permute-start | bytes 73736 | tf_op jit(solution)/shard_map/while/body/eval_jaxpr/ppermute | solution.py:17
  194.7 5.7 %collective-permute-start = (f32[3,2,1024]{2,1,0:T(2,128)}, f32[3,2,1024]{2,1,0:T(2,128)S(1)}, u32[]{:S(2)}, u32[]{:S(2)}) collective-permute-start(f32[3,2,1024]{2,1,0:T(2,128)} %get-tuple-element.194), channel_id=1, source_target_pairs={{1,0},{2,1},{3,2},{4,3},{5,4},{6,5},{7,6},{8,7},{9,8},{10,9},{11,1... | collective-permute-start | bytes 73736 | tf_op jit(solution)/shard_map/while/body/eval_jaxpr/ppermute | solution.py:19
  197.5 6.5 %collective-permute-start.1 = (f32[3,2,1024]{2,1,0:T(2,128)}, f32[3,2,1024]{2,1,0:T(2,128)}, u32[]{:S(2)}, u32[]{:S(2)}) collective-permute-start(f32[3,2,1024]{2,1,0:T(2,128)} %get-tuple-element.195), channel_id=1, source_target_pairs={{0,1},{1,2},{2,3},{3,4},{4,5},{5,6},{6,7},{7,8},{8,9},{9,10},{10,1... | collective-permute-start | bytes 73736 | tf_op jit(solution)/shard_map/while/body/eval_jaxpr/ppermute | solution.py:17
  209.1 5.7 %collective-permute-start = (f32[3,2,1024]{2,1,0:T(2,128)}, f32[3,2,1024]{2,1,0:T(2,128)S(1)}, u32[]{:S(2)}, u32[]{:S(2)}) collective-permute-start(f32[3,2,1024]{2,1,0:T(2,128)} %get-tuple-element.194), channel_id=1, source_target_pairs={{1,0},{2,1},{3,2},{4,3},{5,4},{6,5},{7,6},{8,7},{9,8},{10,9},{11,1... | collective-permute-start | bytes 73736 | tf_op jit(solution)/shard_map/while/body/eval_jaxpr/ppermute | solution.py:19
  212.0 6.5 %collective-permute-start.1 = (f32[3,2,1024]{2,1,0:T(2,128)}, f32[3,2,1024]{2,1,0:T(2,128)}, u32[]{:S(2)}, u32[]{:S(2)}) collective-permute-start(f32[3,2,1024]{2,1,0:T(2,128)} %get-tuple-element.195), channel_id=1, source_target_pairs={{0,1},{1,2},{2,3},{3,4},{4,5},{5,6},{6,7},{7,8},{8,9},{9,10},{10,1... | collective-permute-start | bytes 73736 | tf_op jit(solution)/shard_map/while/body/eval_jaxpr/ppermute | solution.py:17
  223.6 5.7 %collective-permute-start = (f32[3,2,1024]{2,1,0:T(2,128)}, f32[3,2,1024]{2,1,0:T(2,128)S(1)}, u32[]{:S(2)}, u32[]{:S(2)}) collective-permute-start(f32[3,2,1024]{2,1,0:T(2,128)} %get-tuple-element.194), channel_id=1, source_target_pairs={{1,0},{2,1},{3,2},{4,3},{5,4},{6,5},{7,6},{8,7},{9,8},{10,9},{11,1... | collective-permute-start | bytes 73736 | tf_op jit(solution)/shard_map/while/body/eval_jaxpr/ppermute | solution.py:19
  226.4 6.5 %collective-permute-start.1 = (f32[3,2,1024]{2,1,0:T(2,128)}, f32[3,2,1024]{2,1,0:T(2,128)}, u32[]{:S(2)}, u32[]{:S(2)}) collective-permute-start(f32[3,2,1024]{2,1,0:T(2,128)} %get-tuple-element.195), channel_id=1, source_target_pairs={{0,1},{1,2},{2,3},{3,4},{4,5},{5,6},{6,7},{7,8},{8,9},{9,10},{10,1... | collective-permute-start | bytes 73736 | tf_op jit(solution)/shard_map/while/body/eval_jaxpr/ppermute | solution.py:17
  238.0 5.7 %collective-permute-start = (f32[3,2,1024]{2,1,0:T(2,128)}, f32[3,2,1024]{2,1,0:T(2,128)S(1)}, u32[]{:S(2)}, u32[]{:S(2)}) collective-permute-start(f32[3,2,1024]{2,1,0:T(2,128)} %get-tuple-element.194), channel_id=1, source_target_pairs={{1,0},{2,1},{3,2},{4,3},{5,4},{6,5},{7,6},{8,7},{9,8},{10,9},{11,1... | collective-permute-start | bytes 73736 | tf_op jit(solution)/shard_map/while/body/eval_jaxpr/ppermute | solution.py:19
  240.9 6.5 %collective-permute-start.1 = (f32[3,2,1024]{2,1,0:T(2,128)}, f32[3,2,1024]{2,1,0:T(2,128)}, u32[]{:S(2)}, u32[]{:S(2)}) collective-permute-start(f32[3,2,1024]{2,1,0:T(2,128)} %get-tuple-element.195), channel_id=1, source_target_pairs={{0,1},{1,2},{2,3},{3,4},{4,5},{5,6},{6,7},{7,8},{8,9},{9,10},{10,1... | collective-permute-start | bytes 73736 | tf_op jit(solution)/shard_map/while/body/eval_jaxpr/ppermute | solution.py:17
  252.5 5.7 %collective-permute-start = (f32[3,2,1024]{2,1,0:T(2,128)}, f32[3,2,1024]{2,1,0:T(2,128)S(1)}, u32[]{:S(2)}, u32[]{:S(2)}) collective-permute-start(f32[3,2,1024]{2,1,0:T(2,128)} %get-tuple-element.194), channel_id=1, source_target_pairs={{1,0},{2,1},{3,2},{4,3},{5,4},{6,5},{7,6},{8,7},{9,8},{10,9},{11,1... | collective-permute-start | bytes 73736 | tf_op jit(solution)/shard_map/while/body/eval_jaxpr/ppermute | solution.py:19
  255.4 6.5 %collective-permute-start.1 = (f32[3,2,1024]{2,1,0:T(2,128)}, f32[3,2,1024]{2,1,0:T(2,128)}, u32[]{:S(2)}, u32[]{:S(2)}) collective-permute-start(f32[3,2,1024]{2,1,0:T(2,128)} %get-tuple-element.195), channel_id=1, source_target_pairs={{0,1},{1,2},{2,3},{3,4},{4,5},{5,6},{6,7},{7,8},{8,9},{9,10},{10,1... | collective-permute-start | bytes 73736 | tf_op jit(solution)/shard_map/while/body/eval_jaxpr/ppermute | solution.py:17
  267.0 5.7 %collective-permute-start = (f32[3,2,1024]{2,1,0:T(2,128)}, f32[3,2,1024]{2,1,0:T(2,128)S(1)}, u32[]{:S(2)}, u32[]{:S(2)}) collective-permute-start(f32[3,2,1024]{2,1,0:T(2,128)} %get-tuple-element.194), channel_id=1, source_target_pairs={{1,0},{2,1},{3,2},{4,3},{5,4},{6,5},{7,6},{8,7},{9,8},{10,9},{11,1... | collective-permute-start | bytes 73736 | tf_op jit(solution)/shard_map/while/body/eval_jaxpr/ppermute | solution.py:19
  269.8 6.5 %collective-permute-start.1 = (f32[3,2,1024]{2,1,0:T(2,128)}, f32[3,2,1024]{2,1,0:T(2,128)}, u32[]{:S(2)}, u32[]{:S(2)}) collective-permute-start(f32[3,2,1024]{2,1,0:T(2,128)} %get-tuple-element.195), channel_id=1, source_target_pairs={{0,1},{1,2},{2,3},{3,4},{4,5},{5,6},{6,7},{7,8},{8,9},{9,10},{10,1... | collective-permute-start | bytes 73736 | tf_op jit(solution)/shard_map/while/body/eval_jaxpr/ppermute | solution.py:17
  281.4 5.7 %collective-permute-start = (f32[3,2,1024]{2,1,0:T(2,128)}, f32[3,2,1024]{2,1,0:T(2,128)S(1)}, u32[]{:S(2)}, u32[]{:S(2)}) collective-permute-start(f32[3,2,1024]{2,1,0:T(2,128)} %get-tuple-element.194), channel_id=1, source_target_pairs={{1,0},{2,1},{3,2},{4,3},{5,4},{6,5},{7,6},{8,7},{9,8},{10,9},{11,1... | collective-permute-start | bytes 73736 | tf_op jit(solution)/shard_map/while/body/eval_jaxpr/ppermute | solution.py:19
  284.3 6.5 %collective-permute-start.1 = (f32[3,2,1024]{2,1,0:T(2,128)}, f32[3,2,1024]{2,1,0:T(2,128)}, u32[]{:S(2)}, u32[]{:S(2)}) collective-permute-start(f32[3,2,1024]{2,1,0:T(2,128)} %get-tuple-element.195), channel_id=1, source_target_pairs={{0,1},{1,2},{2,3},{3,4},{4,5},{5,6},{6,7},{7,8},{8,9},{9,10},{10,1... | collective-permute-start | bytes 73736 | tf_op jit(solution)/shard_map/while/body/eval_jaxpr/ppermute | solution.py:17
  295.9 5.7 %collective-permute-start = (f32[3,2,1024]{2,1,0:T(2,128)}, f32[3,2,1024]{2,1,0:T(2,128)S(1)}, u32[]{:S(2)}, u32[]{:S(2)}) collective-permute-start(f32[3,2,1024]{2,1,0:T(2,128)} %get-tuple-element.194), channel_id=1, source_target_pairs={{1,0},{2,1},{3,2},{4,3},{5,4},{6,5},{7,6},{8,7},{9,8},{10,9},{11,1... | collective-permute-start | bytes 73736 | tf_op jit(solution)/shard_map/while/body/eval_jaxpr/ppermute | solution.py:19
  298.7 6.5 %collective-permute-start.1 = (f32[3,2,1024]{2,1,0:T(2,128)}, f32[3,2,1024]{2,1,0:T(2,128)}, u32[]{:S(2)}, u32[]{:S(2)}) collective-permute-start(f32[3,2,1024]{2,1,0:T(2,128)} %get-tuple-element.195), channel_id=1, source_target_pairs={{0,1},{1,2},{2,3},{3,4},{4,5},{5,6},{6,7},{7,8},{8,9},{9,10},{10,1... | collective-permute-start | bytes 73736 | tf_op jit(solution)/shard_map/while/body/eval_jaxpr/ppermute | solution.py:17
  311.1 14.4 %copy-start.4 = (f32[129,1,128]{2,1,0:T(1,128)S(1)}, f32[129,1,128]{2,1,0:T(1,128)}, u32[]{:S(2)}) copy-start(f32[129,1,128]{2,1,0:T(1,128)} %copy-done.3) | copy-start | bytes 198148
  311.1 14.4 %copy-start.6 = (f32[129,1,128]{2,1,0:T(1,128)S(1)}, f32[129,1,128]{2,1,0:T(1,128)}, u32[]{:S(2)}) copy-start(f32[129,1,128]{2,1,0:T(1,128)} %copy-done.5) | copy-start | bytes 198148
  318.0 14.1 %all-to-all-start.1 = ((f32[8,1,2560]{2,1,0:T(1,128)}), f32[8,1,2560]{2,1,0:T(1,128)}, u32[]{:S(2)}, u32[]{:S(2)}) async-start(f32[8,1,2560]{2,1,0:T(1,128)} %reshape.63), calls=%async_computation.1 | async-start | bytes 163840 | tf_op jit(solution)/shard_map/all_to_all | solution.py:155
  (9 other events, 27.8 us)
where the time goes:
time: 361 us; the launch traced here: 354 us
  other arithmetic  109 us (30%)
  starting transfers between devices  85.6 us (24%)
  local copies, waits for them, and re-layouts  81 us (22%)
  waiting for transfers between devices  76.9 us (21%)
    ppermute x19, waiting for transfers between devices, padded(): lax.ppermute(tail, axis, [(i, (i + 1) % count) for i in range(count)])  65.3 us
    ppermute x19, starting transfers between devices, padded(): lax.ppermute(head, axis, [((i + 1) % count, i) for i in range(count)])  55.6 us
    another operation x48, other arithmetic, block(): return (jnp.stack([eta, vel_u, vel_v]), total)  30.2 us
    squeeze x16, local copies, waits for them, and re-layouts, block(): depth, force_u, force_v = (ext_static[0], ext_static[1], ext_static[2])  23.1 us
    add x16, other arithmetic, block(): total = total + jnp.stack([vel_u, vel_v])  21.4 us
    slice x19, local copies, waits for them, and re-layouts, padded(): lax.slice_in_dim(cells, cells.shape[dim] - width, cells.shape[dim], axis=...  18 us
    concatenate x18, other arithmetic, padded(): jnp.concatenate([lax.ppermute(tail, axis, [(i, (i + 1) % count) for i in...  16.3 us
    ppermute x19, starting transfers between devices, padded(): lax.ppermute(tail, axis, [(i, (i + 1) % count) for i in range(count)])  14.4 us
  transfers between devices with their start and end apart: 40, of which 22 were waited for; matrix products, arithmetic and copies ran while one was open for 14% of the time, Pallas kernels for 0%

commit v1 on v0

v1 whole, which is shorter than its diff:
```python
import functools

import jax
import jax.numpy as jnp
from jax import lax
from jax.experimental import pallas as pl
from jax.experimental.pallas import tpu as pltpu
from jax.sharding import PartitionSpec as P

MESH = pl.DeviceIdType.MESH
NSUB = 16
TX = 32
TY = 128
EAST, WEST, NORTH, SOUTH = 0, 1, 2, 3


def iota(shape, dim):
    return lax.broadcasted_iota(jnp.int32, shape, dim)


def turn(a, shift, axis):
    return pltpu.roll(a, shift % a.shape[axis], axis)


def kernel(
    levels_n,
    ocean_hbm,
    baro_hbm,
    lev_hbm,
    out_ref,
    baro_out,
    oc,
    lev_i,
    flat2d,
    rim_out,
    rim_in,
    row_out,
    row_in,
    col_out,
    col_in,
    force,
    frim_out,
    frim_in,
    local_sem,
    send_sem,
    recv_sem,
):
    kk = levels_n
    gx = lax.axis_index("gx")
    gy = lax.axis_index("gy")
    nx = lax.axis_size("gx")
    ny = lax.axis_size("gy")
    xe = lax.rem(gx + 1, nx)
    xw = lax.rem(gx + nx - 1, nx)
    yn = lax.rem(gy + 1, ny)
    ys = lax.rem(gy + ny - 1, ny)
    around = [(x, y) for y in (yn, ys) for x in (xw, gx, xe)]
    everyone = around + [(xw, gy), (xe, gy)]

    barrier = pltpu.get_barrier_semaphore()
    for dev in everyone:
        pl.semaphore_signal(barrier, inc=1, device_id=dev, device_id_type=MESH)

    load_o = pltpu.make_async_copy(ocean_hbm, oc, local_sem.at[0])
    load_b = pltpu.make_async_copy(baro_hbm, flat2d.at[pl.ds(0, 3), pl.ds(TX, TX), :], local_sem.at[1])
    load_l = pltpu.make_async_copy(lev_hbm, lev_i, local_sem.at[2])
    load_o.start()
    load_b.start()
    load_l.start()

    lane = iota((TX, TY), 1)
    row = iota((TX, TY), 0)

    def send(src, dst, index, dev):
        copy = pltpu.make_async_remote_copy(
            src_ref=src,
            dst_ref=dst,
            send_sem=send_sem.at[index],
            recv_sem=recv_sem.at[index],
            device_id=dev,
            device_id_type=MESH,
        )
        copy.start()
        return copy

    load_l.wait()
    lev = lev_i[...].astype(jnp.float32)
    flat2d[3, pl.ds(TX, TX), :] = lev
    load_b.wait()
    quad = [flat2d[f, pl.ds(TX, TX), :] for f in range(4)]
    north = quad[3]
    south = quad[0]
    for f in range(4):
        if f != 3:
            north = jnp.where(lane // 32 == f, turn(quad[f], 32 * (f + 1), 1), north)
        if f != 0:
            south = jnp.where(lane // 32 == f, turn(quad[f], 32 * f, 1), south)
    rim_out[0] = north
    rim_out[1] = south

    load_o.wait()
    row_out[EAST] = oc[pl.ds(0, 4 * kk, stride=TX), :]
    row_out[WEST] = oc[pl.ds(TX - 1, 4 * kk, stride=TX), :]

    step = 8

    def gather_columns(o, carry):
        first, last = carry
        for j in range(step):
            i = o * step + j
            moved = pltpu.roll(oc[pl.ds(pl.multiple_of(i * TX, TX), TX), :], i, 1)
            first = jnp.where(lane == i, moved, first)
            last = jnp.where(lane == lax.rem(i + TY - 1, TY), moved, last)
        return first, last

    zero = jnp.zeros((TX, TY), jnp.float32)
    first, last = lax.fori_loop(0, 4 * kk // step, gather_columns, (zero, zero))
    col_out[0] = first
    col_out[1] = last

    pl.semaphore_wait(barrier, len(everyone))
    copies = [
        send(col_out.at[0], col_in.at[0], 0, (gx, ys)),
        send(col_out.at[1], col_in.at[1], 1, (gx, yn)),
        send(row_out.at[EAST], row_in.at[EAST], 2, (xw, gy)),
        send(row_out.at[WEST], row_in.at[WEST], 3, (xe, gy)),
        send(flat2d.at[:, pl.ds(TX, TX), :], flat2d.at[:, pl.ds(2 * TX, TX), :], 4, (xw, gy)),
        send(flat2d.at[:, pl.ds(TX, TX), :], flat2d.at[:, pl.ds(0, TX), :], 5, (xe, gy)),
    ]
    for s, y in ((0, ys), (1, yn)):
        for j, x in ((0, xe), (1, gx), (2, xw)):
            copies.append(send(rim_out.at[1 - s], rim_in.at[3 * s + j], 6 + 3 * s + j, (x, y)))
    for copy in copies:
        copy.wait()

    top = row == TX - 1
    bottom = row == 0

    def unpack(refs_in, f, start):
        a = turn(refs_in[start], -32 * f, 1)
        b = turn(refs_in[start + 3], 96 - 32 * f, 1)
        return jnp.where(lane < 32, a, jnp.where(lane >= 96, b, 0.0))

    lev_d = unpack(rim_in, 3, 1)
    lev_e = jnp.where(top, flat2d[3, pl.ds(2 * TX, 1), :], turn(lev, -1, 0))
    lev_w = jnp.where(bottom, flat2d[3, pl.ds(TX - 1, 1), :], turn(lev, 1, 0))
    lev_n = jnp.where(lane == TY - 1, turn(lev_d, -1, 1), turn(lev, -1, 1))
    lev_s = jnp.where(lane == 0, turn(lev_d, 1, 1), turn(lev, 1, 1))
    face_e = jnp.minimum(lev, lev_e)
    face_w = jnp.minimum(lev, lev_w)
    face_n = jnp.minimum(lev, lev_n)
    face_s = jnp.minimum(lev, lev_s)
    inverse = 1.0 / jnp.maximum(lev, 1.0)

    row_total = (ny * TY).astype(jnp.float32) if hasattr(ny, "astype") else float(ny * TY)
    y_own = (gy * TY + lane).astype(jnp.float32)
    fcor = 0.5 * (2.0 * (y_own + 0.5) / row_total - 1.0)

    def read(f, k):
        return oc[pl.ds(pl.multiple_of((f * kk + k) * TX, TX), TX), :]

    def rims(f, k):
        i = f * kk + k
        east = row_in[EAST, pl.ds(i, 1), :]
        west = row_in[WEST, pl.ds(i, 1), :]
        back = lax.rem(TY - i, TY)
        return east, west, pltpu.roll(col_in[0], back, 1), pltpu.roll(col_in[1], back, 1)

    def jumps(q, rim, faces):
        east, west, north, south = rim
        qe = jnp.where(top, east, turn(q, -1, 0))
        qw = jnp.where(bottom, west, turn(q, 1, 0))
        qn = turn(jnp.where(lane == 0, north, q), -1, 1)
        qs = turn(jnp.where(lane == TY - 1, south, q), 1, 1)
        return [jnp.where(m, n - q, 0.0) for m, n in zip(faces, (qe, qw, qn, qs))]

    def faces_at(level):
        return [level < m for m in (face_e, face_w, face_n, face_s)]

    def momentum(k, carry):
        press, press_e, press_w, press_n, press_s, sum_u, sum_v, col_u, col_v = carry
        level = k.astype(jnp.float32)
        wet = level < lev
        faces = faces_at(level)
        u = read(0, k)
        v = read(1, k)
        t_rim = rims(2, k)
        s_rim = rims(3, k)

        def add(p, m, s, t):
            return p + jnp.where(m, 0.1 * s - 0.2 * t, 0.0)

        press = add(press, wet, read(3, k), read(2, k))
        press_e = add(press_e, level < edge_e, s_rim[0], t_rim[0])
        press_w = add(press_w, level < edge_w, s_rim[1], t_rim[1])
        press_n = add(press_n, level < lev_d, s_rim[2], t_rim[2])
        press_s = add(press_s, level < lev_d, s_rim[3], t_rim[3])
        pe, pw, pn, ps = jumps(press, (press_e, press_w, press_n, press_s), faces)
        ue, uw, un, us = jumps(u, rims(0, k), faces)
        ve, vw, vn, vs = jumps(v, rims(1, k), faces)
        tend_u = (ue + uw) + (un + us) + fcor * v - 0.5 * (pe - pw)
        tend_v = (ve + vw) + (vn + vs) - fcor * u - 0.5 * (pn - ps)
        star_u = u + 0.1 * tend_u
        star_v = v + 0.1 * tend_v
        out_ref[pl.ds(pl.multiple_of(k * TX, TX), TX), :] = star_u
        out_ref[pl.ds(pl.multiple_of((kk + k) * TX, TX), TX), :] = star_v
        return (
            press,
            press_e,
            press_w,
            press_n,
            press_s,
            sum_u + jnp.where(wet, tend_u, 0.0),
            sum_v + jnp.where(wet, tend_v, 0.0),
            col_u + jnp.where(wet, star_u, 0.0),
            col_v + jnp.where(wet, star_v, 0.0),
        )

    edge_e = flat2d[3, pl.ds(2 * TX, 1), :]
    edge_w = flat2d[3, pl.ds(TX - 1, 1), :]
    line = jnp.zeros((1, TY), jnp.float32)
    sums = lax.fori_loop(0, kk, momentum, (zero, line, line, zero, zero, zero, zero, zero, zero))
    force_u = sums[5] * inverse
    force_v = sums[6] * inverse
    mean_u = sums[7] * inverse
    mean_v = sums[8] * inverse
    force[0, pl.ds(TX, TX), :] = force_u
    force[1, pl.ds(TX, TX), :] = force_v

    half = TX // 2
    lane_h = iota((half, TY), 1)
    parts = [a[h * half : (h + 1) * half] for a in (force_u, force_v) for h in (0, 1)]
    north = parts[3]
    south = parts[0]
    for f in range(4):
        if f != 3:
            north = jnp.where(lane_h // 32 == f, turn(parts[f], 32 * (f + 1), 1), north)
        if f != 0:
            south = jnp.where(lane_h // 32 == f, turn(parts[f], 32 * f, 1), south)
    frim_out[0] = north
    frim_out[1] = south
    copies = []
    for s, y in ((0, ys), (1, yn)):
        for j, x in ((0, xe), (1, gx), (2, xw)):
            copies.append(send(frim_out.at[1 - s], frim_in.at[3 * s + j], 14 + 3 * s + j, (x, y)))
    own = force.at[:, pl.ds(TX, TX), :]
    copies.append(send(own, force.at[:, pl.ds(2 * TX, TX), :], 12, (xw, gy)))
    copies.append(send(own, force.at[:, pl.ds(0, TX), :], 13, (xe, gy)))

    def tracers(k, carry):
        level = k.astype(jnp.float32)
        wet = level < lev
        faces = faces_at(level)
        u = 0.05 * read(0, k)
        v = 0.05 * read(1, k)
        for f in (2, 3):
            q = read(f, k)
            je, jw, jn, js = jumps(q, rims(f, k), faces)
            new = q + (0.1 * ((je + jw) + (jn + js)) - (u * (je - jw) + v * (jn - js)))
            out_ref[pl.ds(pl.multiple_of((f * kk + k) * TX, TX), TX), :] = jnp.where(wet, new, 0.0)
        return carry

    lax.fori_loop(0, kk, tracers, 0)

    state_d = [
        jnp.concatenate([unpack(rim_in, f, j) for j in range(3)], axis=0) for f in range(4)
    ]
    for copy in copies:
        copy.wait()

    def unpack_half(f, start):
        halves = []
        for h in (0, 1):
            at = 32 * (2 * f + h)
            a = turn(frim_in[start], -at, 1)
            b = turn(frim_in[start + 3], 96 - at, 1)
            halves.append(jnp.where(lane_h < 32, a, jnp.where(lane_h >= 96, b, 0.0)))
        return halves

    force_d = [
        jnp.concatenate([h for j in range(3) for h in unpack_half(f, j)], axis=0) for f in range(2)
    ]

    wide = 3 * TX
    lane_w = iota((wide, TY), 1)
    state = [(flat2d[f], state_d[f]) for f in range(4)]
    wet = [(a > 0.0).astype(jnp.float32) for a in state[3]]
    depth = [a * (1.0 / kk) for a in state[3]]

    def east(a):
        return [turn(x, -1, 0) for x in a]

    def west(a):
        return [turn(x, 1, 0) for x in a]

    def meridional(a, shift, at):
        c, d = [turn(x, shift, 1) for x in a]
        edge = iota(c.shape, 1) == at
        return [jnp.where(edge, d, c), jnp.where(edge, c, d)]

    def north_of(a):
        return meridional(a, -1, TY - 1)

    def south_of(a):
        return meridional(a, 1, 0)

    def both(fn, *args):
        return [fn(*pair) for pair in zip(*args)]

    times = lambda a, b: a * b
    coef_e = both(lambda a, b: 0.15 * a * b, wet, east(wet))
    coef_n = both(lambda a, b: 0.15 * a * b, wet, north_of(wet))
    y_d = lax.rem(gy * TY + lane_w + jnp.where(lane_w < TY // 2, TY, -TY) + ny * TY, ny * TY)
    cor = [
        0.15 * (2.0 * ((gy * TY + lane_w).astype(jnp.float32) + 0.5) / row_total - 1.0),
        0.15 * (2.0 * (y_d.astype(jnp.float32) + 0.5) / row_total - 1.0),
    ]
    eta = both(times, wet, state[0])
    vel_u = both(times, wet, state[1])
    vel_v = both(times, wet, state[2])
    push_u = both(lambda w, a: 0.3 * w * a, wet, (force[0], force_d[0]))
    push_v = both(lambda w, a: 0.3 * w * a, wet, (force[1], force_d[1]))
    total_u = zero
    total_v = zero

    per = NSUB // 4
    for group in range(4):
        if group:
            cut = lambda pair: [a[8 : a.shape[0] - 8] for a in pair]
            eta, vel_u, vel_v, push_u, push_v, coef_e, coef_n, cor, depth = [
                cut(a) for a in (eta, vel_u, vel_v, push_u, push_v, coef_e, coef_n, cor, depth)
            ]
        here = TX - 8 * group

        def substep(_, carry):
            eta, vel_u, vel_v, total_u, total_v = carry
            flow_u = both(times, depth, vel_u)
            flow_v = both(times, depth, vel_v)
            flux_e = both(lambda c, a, b: c * (a + b), coef_e, flow_u, east(flow_u))
            flux_n = both(lambda c, a, b: c * (a + b), coef_n, flow_v, north_of(flow_v))
            eta = both(
                lambda h, e, w, n, s: h - ((e - w) + (n - s)),
                eta,
                flux_e,
                west(flux_e),
                flux_n,
                south_of(flux_n),
            )
            grad_e = both(lambda c, a, b: c * (b - a), coef_e, eta, east(eta))
            grad_n = both(lambda c, a, b: c * (b - a), coef_n, eta, north_of(eta))
            new_u = both(
                lambda u, v, f, p, a, b: (u - (a + b)) + (f * v + p),
                vel_u,
                vel_v,
                cor,
                push_u,
                grad_e,
                west(grad_e),
            )
            new_v = both(
                lambda v, u, f, p, a, b: (v - (a + b)) - (f * u - p),
                vel_v,
                vel_u,
                cor,
                push_v,
                grad_n,
                south_of(grad_n),
            )
            total_u = total_u + new_u[0][here : here + TX]
            total_v = total_v + new_v[0][here : here + TX]
            return eta, new_u, new_v, total_u, total_v

        eta, vel_u, vel_v, total_u, total_v = lax.fori_loop(
            0, per, substep, (eta, vel_u, vel_v, total_u, total_v)
        )

    for f, a in enumerate((eta, vel_u, vel_v)):
        baro_out[f] = a[0][8 : 8 + TX]
    shift_u = total_u * (1.0 / NSUB) - mean_u
    shift_v = total_v * (1.0 / NSUB) - mean_v

    def finish(k, carry):
        is_wet = k.astype(jnp.float32) < lev
        for f, shift in ((0, shift_u), (1, shift_v)):
            at = pl.ds(pl.multiple_of((f * kk + k) * TX, TX), TX)
            out_ref[at, :] = jnp.where(is_wet, out_ref[at, :] + shift, 0.0)
        return carry

    lax.fori_loop(0, kk, finish, 0)


def per_device(ocean_state, barotropic, levels):
    kk = ocean_state.shape[1]
    rows = 4 * kk * TX
    f32 = jnp.float32
    new, baro = pl.pallas_call(
        functools.partial(kernel, kk),
        out_shape=(
            jax.ShapeDtypeStruct((rows, TY), f32),
            jax.ShapeDtypeStruct((3, TX, TY), f32),
        ),
        in_specs=[pl.BlockSpec(memory_space=pl.ANY)] * 3,
        out_specs=(
            pl.BlockSpec(memory_space=pltpu.VMEM),
            pl.BlockSpec(memory_space=pltpu.VMEM),
        ),
        scratch_shapes=[
            pltpu.VMEM((rows, TY), f32),
            pltpu.VMEM((TX, TY), jnp.int32),
            pltpu.VMEM((4, 3 * TX, TY), f32),
            pltpu.VMEM((2, TX, TY), f32),
            pltpu.VMEM((6, TX, TY), f32),
            pltpu.VMEM((2, 4 * kk, TY), f32),
            pltpu.VMEM((2, 4 * kk, TY), f32),
            pltpu.VMEM((2, TX, TY), f32),
            pltpu.VMEM((2, TX, TY), f32),
            pltpu.VMEM((2, 3 * TX, TY), f32),
            pltpu.VMEM((2, TX // 2, TY), f32),
            pltpu.VMEM((6, TX // 2, TY), f32),
            pltpu.SemaphoreType.DMA((3,)),
            pltpu.SemaphoreType.DMA((20,)),
            pltpu.SemaphoreType.DMA((20,)),
        ],
        compiler_params=pltpu.CompilerParams(
            collective_id=0, has_side_effects=True, vmem_limit_bytes=32 * 1024 * 1024
        ),
    )(ocean_state.reshape(rows, TY), barotropic, levels)
    return new.reshape(ocean_state.shape), baro


def solution(mesh):
    in_specs = (P(None, None, "gx", "gy"), P(None, "gx", "gy"), P("gx", "gy"))
    out_specs = (P(None, None, "gx", "gy"), P(None, "gx", "gy"))
    return jax.shard_map(
        per_device, mesh=mesh, in_specs=in_specs, out_specs=out_specs, check_vma=False
    )
```

time: 361 us -> 40.7 us (0.11)
  the two profiles are of different devices: /device:TPU:8 before, /device:TPU:1 now
where the time goes in v1:
time: 40.7 us; the launch traced here: 40.5 us
  Pallas kernels  34.8 us (86%)
  local copies, waits for them, and re-layouts  5.04 us (12%)
  between operations  0.65 us (2%)
    pallas_call x1, Pallas kernels, per_device(): pl.pallas_call(functools.partial(kernel, kk), out_shape=(jax.ShapeDtypeSt...  34.8 us
    unnamed x8, local copies, waits for them, and re-layouts  5.04 us

profile of v1, /device:TPU:1, one launch (start us, length us, event | category | flops | bytes accessed | tf_op | source)
XLA Modules:
  0.0 40.5 jit_solution(13454224387965027903)
XLA Ops:
  0.6 0.0 copy-start
  0.6 1.6 %copy-done = f32[4,32,32,128]{3,2,1,0:T(8,128)S(1)} copy-done((f32[4,32,32,128]{3,2,1,0:T(8,128)S(1)}, f32[4,32,32,128]{3,2,1,0:T(8,128)}, u32[]{:S(2)}) %copy-start) | copy-done | bytes 2097176
  2.2 0.0 copy-start.1
  2.2 0.8 %copy-done.1 = f32[3,32,128]{2,1,0:T(8,128)S(1)} copy-done((f32[3,32,128]{2,1,0:T(8,128)S(1)}, f32[3,32,128]{2,1,0:T(8,128)}, u32[]{:S(2)}) %copy-start.1) | copy-done | bytes 49176
  3.0 0.0 copy-start.2
  3.0 0.7 %copy-done.2 = s32[32,128]{1,0:T(8,128)S(1)} copy-done((s32[32,128]{1,0:T(8,128)S(1)}, s32[32,128]{1,0:T(8,128)}, u32[]{:S(2)}) %copy-start.2) | copy-done | bytes 16408
  3.7 34.8 %shard_map.50 = (f32[4096,128]{1,0:T(8,128)S(1)}, f32[3,32,128]{2,1,0:T(8,128)S(1)}) custom-call(f32[4096,128]{1,0:T(8,128)S(1)} %bitcast.2, f32[3,32,128]{2,1,0:T(8,128)S(1)} %copy-done.1, s32[32,128]{1,0:T(8,128)S(1)} %copy-done.2), custom_call_target="tpu_custom_call" | custom-call | tf_op jit(solution)/shard_map/pallas_call | solution.py:396
  38.6 1.3 %copy.7 = f32[4,32,32,128]{3,2,1,0:T(8,128)} copy(f32[4,32,32,128]{3,2,1,0:T(8,128)S(1)} %bitcast.3) | data formatting | bytes 4194304
  39.9 0.6 %copy.8 = f32[3,32,128]{2,1,0:T(8,128)} copy(f32[3,32,128]{2,1,0:T(8,128)S(1)} %get-tuple-element.9) | data formatting | bytes 98304
Async XLA Ops:
  0.6 1.6 %copy-start = (f32[4,32,32,128]{3,2,1,0:T(8,128)S(1)}, f32[4,32,32,128]{3,2,1,0:T(8,128)}, u32[]{:S(2)}) copy-start(f32[4,32,32,128]{3,2,1,0:T(8,128)} %param.3) | copy-start | bytes 6291460
  2.2 0.8 %copy-start.1 = (f32[3,32,128]{2,1,0:T(8,128)S(1)}, f32[3,32,128]{2,1,0:T(8,128)}, u32[]{:S(2)}) copy-start(f32[3,32,128]{2,1,0:T(8,128)} %baro_hbm.1) | copy-start | bytes 147460
  3.0 0.7 %copy-start.2 = (s32[32,128]{1,0:T(8,128)S(1)}, s32[32,128]{1,0:T(8,128)}, u32[]{:S(2)}) copy-start(s32[32,128]{1,0:T(8,128)} %lev_hbm.1) | copy-start | bytes 49156

commit v2 on v1

v2 whole, which is shorter than its diff:
```python
import functools

import jax
import jax.numpy as jnp
from jax import lax
from jax.experimental import pallas as pl
from jax.experimental.pallas import tpu as pltpu
from jax.sharding import PartitionSpec as P

MESH = pl.DeviceIdType.MESH
NSUB = 16
TX = 32
TY = 128
RIM = 32
F32 = jnp.float32


def iota(shape, dim):
    return lax.broadcasted_iota(jnp.int32, shape, dim)


def turn(a, shift, axis):
    return pltpu.roll(a, shift % a.shape[axis], axis)


def at_level(i):
    return pl.ds(pl.multiple_of(i * TX, TX), TX)


def unrolled(n, times, body, carry):
    def several(o, carry):
        for j in range(times):
            carry = body(o * times + j, carry)
        return carry

    return lax.fori_loop(0, n // times, several, carry)


class Link:
    def __init__(self, copy, sends=None, receives=None):
        self.copy, self.sends, self.receives = copy, sends, receives

    def do(self, what, when):
        if when is None:
            what()
        else:
            pl.when(when)(lambda: what())

    def start(self):
        self.do(self.copy.start, self.sends)

    def wait_send(self):
        self.do(self.copy.wait_send, self.sends)

    def wait_recv(self):
        self.do(self.copy.wait_recv, self.receives)


def pack(parts, lane):
    north, south = parts[3], parts[0]
    for f in range(4):
        if f != 3:
            north = jnp.where(lane // RIM == f, turn(parts[f], RIM * (f + 1), 1), north)
        if f != 0:
            south = jnp.where(lane // RIM == f, turn(parts[f], RIM * f, 1), south)
    return north, south


def unpack(north, south, f, lane):
    a = turn(north, -RIM * f, 1)
    b = turn(south, TY - RIM - RIM * f, 1)
    return jnp.where(lane < RIM, a, jnp.where(lane >= TY - RIM, b, 0.0))


def kernel(
    kk,
    ocean_hbm,
    baro_hbm,
    lev_hbm,
    out_ref,
    baro_out,
    shift_out,
    oc,
    press_ref,
    lev_i,
    flat2d,
    rim_out,
    rim_in,
    row_a_out,
    row_a_in,
    row_b_out,
    row_b_in,
    col_a_out,
    col_a_in,
    col_b_out,
    col_b_in,
    force,
    frim_out,
    frim_in,
    local_sem,
    send_sem,
    recv_sem,
):
    gx = lax.axis_index("gx")
    gy = lax.axis_index("gy")
    nx = lax.axis_size("gx")
    ny = lax.axis_size("gy")
    xe = lax.rem(gx + 1, nx)
    xw = lax.rem(gx + nx - 1, nx)
    yn = lax.rem(gy + 1, ny)
    ys = lax.rem(gy + ny - 1, ny)
    has_n = gy < ny - 1
    has_s = gy > 0

    barrier = pltpu.get_barrier_semaphore()

    def greet(x, y):
        pl.semaphore_signal(barrier, inc=1, device_id=(x, y), device_id_type=MESH)

    @pl.when(has_n)
    def _():
        for x in (xw, xe, gx):
            greet(x, yn)

    @pl.when(has_s)
    def _():
        for x in (xw, xe, gx):
            greet(x, ys)

    greet(xw, gy)
    greet(xe, gy)
    greeted = 2 + 3 * (has_n.astype(jnp.int32) + has_s.astype(jnp.int32))

    load_o = pltpu.make_async_copy(ocean_hbm, oc, local_sem.at[0])
    load_b = pltpu.make_async_copy(baro_hbm, flat2d.at[pl.ds(0, 3), pl.ds(TX, TX), :], local_sem.at[1])
    load_l = pltpu.make_async_copy(lev_hbm, lev_i, local_sem.at[2])
    load_l.start()
    load_b.start()
    load_o.start()

    lane = iota((TX, TY), 1)
    row = iota((TX, TY), 0)
    zero = jnp.zeros((TX, TY), F32)
    counter = [0]

    def link(src, dst, dev, sends=None, receives=None):
        index = counter[0]
        counter[0] += 1
        return Link(
            pltpu.make_async_remote_copy(
                src_ref=src,
                dst_ref=dst,
                send_sem=send_sem.at[index],
                recv_sem=recv_sem.at[index],
                device_id=dev,
                device_id_type=MESH,
            ),
            sends,
            receives,
        )

    def southward(src, dst, x=gx):
        return link(src, dst, (x, ys), has_s, has_n)

    def northward(src, dst, x=gx):
        return link(src, dst, (x, yn), has_n, has_s)

    def westward(src, dst):
        return link(src, dst, (xw, gy))

    def eastward(src, dst):
        return link(src, dst, (xe, gy))

    own = pl.ds(TX, TX)
    after = pl.ds(2 * TX, TX)
    before = pl.ds(0, TX)
    links_a = [
        southward(col_a_out.at[0], col_a_in.at[0]),
        northward(col_a_out.at[1], col_a_in.at[1]),
        westward(row_a_out.at[0], row_a_in.at[0]),
        eastward(row_a_out.at[1], row_a_in.at[1]),
    ]
    links_rim = [
        southward(rim_out.at[1], rim_in.at[1]),
        northward(rim_out.at[0], rim_in.at[4]),
    ]
    links_2d = [
        westward(flat2d.at[:, own, :], flat2d.at[:, after, :]),
        eastward(flat2d.at[:, own, :], flat2d.at[:, before, :]),
    ]
    links_b = [
        southward(col_b_out.at[0], col_b_in.at[0]),
        northward(col_b_out.at[1], col_b_in.at[1]),
        westward(row_b_out.at[0], row_b_in.at[0]),
        eastward(row_b_out.at[1], row_b_in.at[1]),
    ]
    links_relay = [
        link(rim_in.at[1], rim_in.at[2], (xw, gy), has_n, has_n),
        link(rim_in.at[1], rim_in.at[0], (xe, gy), has_n, has_n),
        link(rim_in.at[4], rim_in.at[5], (xw, gy), has_s, has_s),
        link(rim_in.at[4], rim_in.at[3], (xe, gy), has_s, has_s),
    ]
    links_force = [
        southward(frim_out.at[1], frim_in.at[0], xe),
        northward(frim_out.at[0], frim_in.at[3], xe),
        southward(frim_out.at[1], frim_in.at[2], xw),
        northward(frim_out.at[0], frim_in.at[5], xw),
        southward(frim_out.at[1], frim_in.at[1]),
        northward(frim_out.at[0], frim_in.at[4]),
        westward(force.at[:, own, :], force.at[:, after, :]),
        eastward(force.at[:, own, :], force.at[:, before, :]),
    ]

    @pl.when(jnp.logical_not(has_n))
    def _():
        rim_in[0:3] = jnp.zeros((3, TX, TY), F32)
        frim_in[0:3] = jnp.zeros((3, TX // 2, TY), F32)

    @pl.when(jnp.logical_not(has_s))
    def _():
        rim_in[3:6] = jnp.zeros((3, TX, TY), F32)
        frim_in[3:6] = jnp.zeros((3, TX // 2, TY), F32)

    load_l.wait()
    lev = lev_i[...].astype(F32)
    flat2d[3, own, :] = lev
    load_b.wait()
    north, south = pack([flat2d[f, own, :] for f in range(4)], lane)
    rim_out[0] = north
    rim_out[1] = south

    load_o.wait()
    for side, x in ((0, 0), (1, TX - 1)):
        row_a_out[side, pl.ds(0, 2 * kk), :] = oc[pl.ds(x, 2 * kk, stride=TX), :]
        row_b_out[side] = oc[pl.ds(2 * kk * TX + x, 2 * kk, stride=TX), :]
        row_a_out[side, pl.ds(3 * kk, 8), :] = jnp.broadcast_to(lev[x : x + 1], (8, TY))

    def gather(k, carry):
        press, first_a, last_a, first_b, last_b = carry
        t = oc[at_level(2 * kk + k), :]
        s = oc[at_level(3 * kk + k), :]
        press = press + jnp.where(k.astype(F32) < lev, 0.1 * s - 0.2 * t, 0.0)
        press_ref[at_level(k), :] = press
        u = oc[at_level(k), :]
        v = oc[at_level(kk + k), :]
        for f, q in ((0, u), (1, v), (2, press)):
            moved = pltpu.roll(q, f * kk + k, 1)
            first_a = jnp.where(lane == f * kk + k, moved, first_a)
            last_a = jnp.where(lane == lax.rem(f * kk + k + TY - 1, TY), moved, last_a)
        for f, q in ((0, t), (1, s)):
            moved = pltpu.roll(q, f * kk + k, 1)
            first_b = jnp.where(lane == f * kk + k, moved, first_b)
            last_b = jnp.where(lane == lax.rem(f * kk + k + TY - 1, TY), moved, last_b)
        return press, first_a, last_a, first_b, last_b

    _, first_a, last_a, first_b, last_b = unrolled(kk, 2, gather, (zero,) * 5)
    last_a = turn(last_a, 1, 1)
    last_b = turn(last_b, 1, 1)
    first_lev = jnp.broadcast_to(lev[:, 0:1], (TX, TY))
    last_lev = jnp.broadcast_to(lev[:, TY - 1 : TY], (TX, TY))
    in_lev = lane >= 96
    col_a_out[0] = jnp.where(in_lev, first_lev, first_a)
    col_a_out[1] = jnp.where(in_lev, last_lev, last_a)
    col_b_out[0] = first_b
    col_b_out[1] = last_b
    for side, x in ((0, 0), (1, TX - 1)):
        row_a_out[side, pl.ds(2 * kk, kk), :] = press_ref[pl.ds(x, kk, stride=TX), :]

    face_e = jnp.where(row == TX - 1, 0.0, jnp.minimum(lev, turn(lev, -1, 0)))
    face_n = jnp.where(lane == TY - 1, 0.0, jnp.minimum(lev, turn(lev, -1, 1)))
    inverse = 1.0 / jnp.maximum(lev, 1.0)
    row_total = float(ny * TY)
    y_own = (gy * TY + lane).astype(F32)
    fcor = 0.5 * (2.0 * (y_own + 0.5) / row_total - 1.0)

    def jumps(q, in_e, in_n):
        e = jnp.where(in_e, turn(q, -1, 0) - q, 0.0)
        n = jnp.where(in_n, turn(q, -1, 1) - q, 0.0)
        return e, turn(e, 1, 0), n, turn(n, 1, 1)

    def momentum(k, carry):
        sum_u, sum_v, col_u, col_v = carry
        level = k.astype(F32)
        wet = level < lev
        in_e = level < face_e
        in_n = level < face_n
        u = oc[at_level(k), :]
        v = oc[at_level(kk + k), :]
        pe, pw, pn, ps = jumps(press_ref[at_level(k), :], in_e, in_n)
        ue, uw, un, us = jumps(u, in_e, in_n)
        ve, vw, vn, vs = jumps(v, in_e, in_n)
        tend_u = ((ue - uw) + (un - us)) + (fcor * v - 0.5 * (pe + pw))
        tend_v = ((ve - vw) + (vn - vs)) - (fcor * u + 0.5 * (pn + ps))
        star_u = u + 0.1 * tend_u
        star_v = v + 0.1 * tend_v
        out_ref[at_level(k), :] = star_u
        out_ref[at_level(kk + k), :] = star_v
        return (
            sum_u + jnp.where(wet, tend_u, 0.0),
            sum_v + jnp.where(wet, tend_v, 0.0),
            col_u + jnp.where(wet, star_u, 0.0),
            col_v + jnp.where(wet, star_v, 0.0),
        )

    def tracers(k, carry):
        level = k.astype(F32)
        wet = level < lev
        in_e = level < face_e
        in_n = level < face_n
        u = 0.05 * oc[at_level(k), :]
        v = 0.05 * oc[at_level(kk + k), :]
        for f in (2, 3):
            q = oc[at_level(f * kk + k), :]
            e, w, n, s = jumps(q, in_e, in_n)
            new = q + (0.1 * ((e - w) + (n - s)) - (u * (e + w) + v * (n + s)))
            out_ref[at_level(f * kk + k), :] = jnp.where(wet, new, 0.0)
        return carry

    sum_u, sum_v, col_u, col_v = unrolled(kk, 2, momentum, (zero,) * 4)

    pl.semaphore_wait(barrier, greeted)
    for x in links_a + links_rim + links_2d + links_b:
        x.start()

    unrolled(kk, 2, tracers, 0)

    for x in links_a:
        x.wait_recv()
    level = iota((kk, TY), 0).astype(F32)
    rows_add = []
    for side, sign in ((0, 1.0), (1, -1.0)):
        mine = row_a_out.at[1 - side]
        theirs = row_a_in.at[side]
        face = jnp.minimum(mine[pl.ds(3 * kk, 1), :], theirs[pl.ds(3 * kk, 1), :])
        wet = level < face
        ju, jv, jp = [
            jnp.where(wet, theirs[pl.ds(f * kk, kk), :] - mine[pl.ds(f * kk, kk), :], 0.0)
            for f in range(3)
        ]
        rows_add.append((wet, ju - (0.5 * sign) * jp, jv))
    cols_add = []
    level_l = jnp.where(lane < kk, lane, jnp.where(lane < 2 * kk, lane - kk, lane - 2 * kk)).astype(F32)
    in_u = lane < kk
    in_v = jnp.logical_and(lane >= kk, lane < 2 * kk)
    in_p = jnp.logical_and(lane >= 2 * kk, lane < 3 * kk)
    for side, sign in ((0, 1.0), (1, -1.0)):
        mine = col_a_out[1 - side]
        theirs = col_a_in[side]
        their_lev = jnp.broadcast_to(theirs[:, TY - 1 : TY], (TX, TY))
        my_lev = last_lev if side == 0 else first_lev
        wet = jnp.logical_and(level_l < jnp.minimum(my_lev, their_lev), (has_n, has_s)[side])
        jump = jnp.where(wet, theirs - mine, 0.0)
        both = jnp.where(in_p, (-0.5 * sign) * jump, jump)
        cols_add.append((wet, both))

    def total(a):
        return jnp.sum(a, axis=0, keepdims=True)

    def across(a, mask):
        return jnp.sum(jnp.where(mask, a, 0.0), axis=1, keepdims=True)

    in_vp = jnp.logical_or(in_v, in_p)
    extra_u = jnp.where(row == TX - 1, total(rows_add[0][1]), 0.0)
    extra_u += jnp.where(row == 0, total(rows_add[1][1]), 0.0)
    extra_u += jnp.where(lane == TY - 1, across(cols_add[0][1], in_u), 0.0)
    extra_u += jnp.where(lane == 0, across(cols_add[1][1], in_u), 0.0)
    extra_v = jnp.where(row == TX - 1, total(rows_add[0][2]), 0.0)
    extra_v += jnp.where(row == 0, total(rows_add[1][2]), 0.0)
    extra_v += jnp.where(lane == TY - 1, across(cols_add[0][1], in_vp), 0.0)
    extra_v += jnp.where(lane == 0, across(cols_add[1][1], in_vp), 0.0)
    force_u = (sum_u + extra_u) * inverse
    force_v = (sum_v + extra_v) * inverse
    force[0, own, :] = force_u
    force[1, own, :] = force_v
    half = TX // 2
    lane_h = iota((half, TY), 1)
    north, south = pack(
        [a[h * half : (h + 1) * half] for a in (force_u, force_v) for h in (0, 1)], lane_h
    )
    frim_out[0] = north
    frim_out[1] = south
    for x in links_force:
        x.start()

    for x in links_rim:
        x.wait_recv()
    for x in links_relay:
        x.start()
    mean_u = (col_u + 0.1 * extra_u) * inverse
    mean_v = (col_v + 0.1 * extra_v) * inverse

    for x in links_b:
        x.wait_recv()
    for side, sign, x in ((0, 1.0, TX - 1), (1, -1.0, 0)):
        wet, add_u, add_v = rows_add[side]
        for f, add in ((0, add_u), (1, add_v)):
            at = pl.ds(f * kk * TX + x, kk, stride=TX)
            out_ref[at, :] = out_ref[at, :] + 0.1 * add
        weight = 0.1 - (0.05 * sign) * row_a_out[1 - side, pl.ds(0, kk), :]
        for f in (0, 1):
            at = pl.ds((2 + f) * kk * TX + x, kk, stride=TX)
            rows = pl.ds(f * kk, kk)
            jump = jnp.where(wet, row_b_in[side, rows, :] - row_b_out[1 - side, rows, :], 0.0)
            out_ref[at, :] = out_ref[at, :] + weight * jump
    patches = []
    for side, sign in ((0, 1.0), (1, -1.0)):
        wet, both = cols_add[side]
        mine = col_a_out[1 - side]
        first = 0.1 * (both + jnp.where(in_v, turn(jnp.where(in_p, both, 0.0), -kk, 1), 0.0))
        v = jnp.where(lane < kk, turn(mine, -kk, 1), mine)
        jump = jnp.where(
            wet,
            col_b_in[side] - col_b_out[1 - side],
            0.0,
        )
        second = (0.1 - (0.05 * sign) * v) * jump
        patch = jnp.where(lane < 2 * kk, first, turn(second, 2 * kk, 1))
        patches.append(patch)
    north, south = turn(patches[0], -1, 1), patches[1]
    odd = lane % 2 == 1
    mixed = [jnp.where(odd, north, south), jnp.where(odd, south, north)]
    outer = jnp.logical_or(lane == 0, lane == TY - 1)

    def patch_columns(o, carry):
        for j in range(4):
            i = o * 4 + j
            add = pltpu.roll(mixed[j % 2], lax.rem(TY - i, TY), 1)
            out_ref[at_level(i), :] = out_ref[at_level(i), :] + jnp.where(outer, add, 0.0)
        return carry

    lax.fori_loop(0, kk, patch_columns, 0)

    for x in links_2d + links_relay:
        x.wait_recv()
    state_d = [
        jnp.concatenate([unpack(rim_in[j], rim_in[3 + j], f, lane) for j in range(3)], axis=0)
        for f in range(4)
    ]
    wide = 3 * TX
    lane_w = iota((wide, TY), 1)
    state = [(flat2d[f], state_d[f]) for f in range(4)]
    wet = [(a > 0.0).astype(F32) for a in state[3]]
    depth = [a * (1.0 / kk) for a in state[3]]

    def east(a):
        return [turn(x, -1, 0) for x in a]

    def west(a):
        return [turn(x, 1, 0) for x in a]

    def meridional(a, shift, at):
        c, d = [turn(x, shift, 1) for x in a]
        edge = iota(c.shape, 1) == at
        return [jnp.where(edge, d, c), jnp.where(edge, c, d)]

    def north_of(a):
        return meridional(a, -1, TY - 1)

    def south_of(a):
        return meridional(a, 1, 0)

    def both(fn, *args):
        return [fn(*pair) for pair in zip(*args)]

    def times(a, b):
        return a * b

    coef_e = both(lambda a, b: 0.15 * a * b, wet, east(wet))
    coef_n = both(lambda a, b: 0.15 * a * b, wet, north_of(wet))
    y_d = lax.rem(gy * TY + lane_w + jnp.where(lane_w < TY // 2, TY, -TY) + ny * TY, ny * TY)
    cor = [
        0.15 * (2.0 * ((gy * TY + lane_w).astype(F32) + 0.5) / row_total - 1.0),
        0.15 * (2.0 * (y_d.astype(F32) + 0.5) / row_total - 1.0),
    ]
    eta = both(times, wet, state[0])
    vel_u = both(times, wet, state[1])
    vel_v = both(times, wet, state[2])

    for x in links_force:
        x.wait_recv()
    force_d = [
        jnp.concatenate(
            [
                unpack(frim_in[j], frim_in[3 + j], 2 * f + h, lane_h)
                for j in range(3)
                for h in (0, 1)
            ],
            axis=0,
        )
        for f in range(2)
    ]
    push_u = both(lambda w, a: 0.3 * w * a, wet, (force[0], force_d[0]))
    push_v = both(lambda w, a: 0.3 * w * a, wet, (force[1], force_d[1]))
    total_u = zero
    total_v = zero

    per = NSUB // 4
    for group in range(4):
        if group:

            def cut(pair):
                return [a[8 : a.shape[0] - 8] for a in pair]

            eta, vel_u, vel_v, push_u, push_v, coef_e, coef_n, cor, depth = [
                cut(a) for a in (eta, vel_u, vel_v, push_u, push_v, coef_e, coef_n, cor, depth)
            ]
        here = TX - 8 * group

        def substep(_, carry):
            eta, vel_u, vel_v, total_u, total_v = carry
            flow_u = both(times, depth, vel_u)
            flow_v = both(times, depth, vel_v)
            flux_e = both(lambda c, a, b: c * (a + b), coef_e, flow_u, east(flow_u))
            flux_n = both(lambda c, a, b: c * (a + b), coef_n, flow_v, north_of(flow_v))
            eta = both(
                lambda h, e, w, n, s: h - ((e - w) + (n - s)),
                eta,
                flux_e,
                west(flux_e),
                flux_n,
                south_of(flux_n),
            )
            grad_e = both(lambda c, a, b: c * (b - a), coef_e, eta, east(eta))
            grad_n = both(lambda c, a, b: c * (b - a), coef_n, eta, north_of(eta))
            new_u = both(
                lambda u, v, f, p, a, b: (u - (a + b)) + (f * v + p),
                vel_u,
                vel_v,
                cor,
                push_u,
                grad_e,
                west(grad_e),
            )
            new_v = both(
                lambda v, u, f, p, a, b: (v - (a + b)) - (f * u - p),
                vel_v,
                vel_u,
                cor,
                push_v,
                grad_n,
                south_of(grad_n),
            )
            total_u = total_u + new_u[0][here : here + TX]
            total_v = total_v + new_v[0][here : here + TX]
            return eta, new_u, new_v, total_u, total_v

        eta, vel_u, vel_v, total_u, total_v = lax.fori_loop(
            0, per, substep, (eta, vel_u, vel_v, total_u, total_v)
        )

    for f, a in enumerate((eta, vel_u, vel_v)):
        baro_out[f] = a[0][8 : 8 + TX]
    shift_out[0] = total_u * (1.0 / NSUB) - mean_u
    shift_out[1] = total_v * (1.0 / NSUB) - mean_v
    shift_out[2] = lev
    for x in links_a + links_rim + links_2d + links_b + links_relay + links_force:
        x.wait_send()


def finish(kk, star, baro, shift, out_hbm, baro_hbm, fast, sems):
    half = 2 * kk * TX
    copies = [
        pltpu.make_async_copy(star.at[pl.ds(half, half), :], out_hbm.at[pl.ds(half, half), :], sems.at[0]),
        pltpu.make_async_copy(baro, baro_hbm, sems.at[1]),
    ]
    for x in copies:
        x.start()
    lev = shift[2]
    for f in (0, 1):
        add = shift[f]

        def body(k, carry):
            i = f * kk + k
            fast[at_level(i), :] = jnp.where(k.astype(F32) < lev, star[at_level(i), :] + add, 0.0)
            return carry

        unrolled(kk, 4, body, 0)
        part = pl.ds(f * kk * TX, kk * TX)
        copies.append(pltpu.make_async_copy(fast.at[part, :], out_hbm.at[part, :], sems.at[2 + f]))
        copies[-1].start()
    for x in copies:
        x.wait()


def per_device(ocean_state, barotropic, levels):
    kk = ocean_state.shape[1]
    rows = 4 * kk * TX
    hbm = pl.BlockSpec(memory_space=pltpu.HBM)
    vmem = pl.BlockSpec(memory_space=pltpu.VMEM)
    links = 24

    def shape(*dims):
        return jax.ShapeDtypeStruct(dims, F32)

    star, baro, shift = pl.pallas_call(
        functools.partial(kernel, kk),
        out_shape=tuple(pltpu.VMEM(d, F32) for d in ((rows, TY), (3, TX, TY), (3, TX, TY))),
        in_specs=[hbm] * 3,
        out_specs=(vmem,) * 3,
        scratch_shapes=[
            pltpu.VMEM((rows, TY), F32),
            pltpu.VMEM((kk * TX, TY), F32),
            pltpu.VMEM((TX, TY), jnp.int32),
            pltpu.VMEM((4, 3 * TX, TY), F32),
            pltpu.VMEM((2, TX, TY), F32),
            pltpu.VMEM((6, TX, TY), F32),
            pltpu.VMEM((2, 3 * kk + 8, TY), F32),
            pltpu.VMEM((2, 3 * kk + 8, TY), F32),
            pltpu.VMEM((2, 2 * kk, TY), F32),
            pltpu.VMEM((2, 2 * kk, TY), F32),
            pltpu.VMEM((2, TX, TY), F32),
            pltpu.VMEM((2, TX, TY), F32),
            pltpu.VMEM((2, TX, TY), F32),
            pltpu.VMEM((2, TX, TY), F32),
            pltpu.VMEM((2, 3 * TX, TY), F32),
            pltpu.VMEM((2, TX // 2, TY), F32),
            pltpu.VMEM((6, TX // 2, TY), F32),
            pltpu.SemaphoreType.DMA((3,)),
            pltpu.SemaphoreType.DMA((links,)),
            pltpu.SemaphoreType.DMA((links,)),
        ],
        compiler_params=pltpu.CompilerParams(
            collective_id=0, has_side_effects=True, vmem_limit_bytes=32 * 1024 * 1024
        ),
        name="ocean_step",
    )(*[pltpu.with_memory_space_constraint(a, pltpu.HBM) for a in (ocean_state.reshape(rows, TY), barotropic, levels)])
    new, baro = pl.pallas_call(
        functools.partial(finish, kk),
        out_shape=(shape(rows, TY), shape(3, TX, TY)),
        in_specs=[vmem] * 3,
        out_specs=(hbm,) * 2,
        scratch_shapes=[
            pltpu.VMEM((2 * kk * TX, TY), F32),
            pltpu.SemaphoreType.DMA((4,)),
        ],
        compiler_params=pltpu.CompilerParams(vmem_limit_bytes=16 * 1024 * 1024),
        name="finish",
    )(star, baro, shift)
    return new.reshape(ocean_state.shape), baro


def solution(mesh):
    in_specs = (P(None, None, "gx", "gy"), P(None, "gx", "gy"), P("gx", "gy"))
    out_specs = (P(None, None, "gx", "gy"), P(None, "gx", "gy"))
    return jax.shard_map(
        per_device, mesh=mesh, in_specs=in_specs, out_specs=out_specs, check_vma=False
    )
```

time: 40.7 us -> 28.8 us (0.71)
  Pallas kernels: 34.8 us -> 28 us
  local copies, waits for them, and re-layouts: 5.04 us -> 0 us
    pallas_call x1 -> x2, Pallas kernels: 34.8 us -> 28 us  [the longest x1 26.6 us: per_device(): pl.pallas_call(functools.partial(kernel, kk), out_shape=tuple((pltpu.VMEM...]
    unnamed x8 -> x0, local copies, waits for them, and re-layouts: 5.04 us -> none
where the time goes in v2:
time: 28.8 us; the launch traced here: 28.6 us
  Pallas kernels  28 us (97%)
  between operations  0.64 us (2%)
    pallas_call x1, Pallas kernels, per_device(): pl.pallas_call(functools.partial(kernel, kk), out_shape=tuple((pltpu.VMEM...  26.6 us
    pallas_call x1, Pallas kernels, per_device(): pl.pallas_call(functools.partial(finish, kk), out_shape=(shape(rows, TY),...  1.37 us

profile of v2, /device:TPU:1, one launch (start us, length us, event | category | flops | bytes accessed | tf_op | source)
XLA Modules:
  0.0 28.6 jit_solution(3475962942475578868)
XLA Ops:
  0.6 26.6 %ocean_step.1 = (f32[4096,128]{1,0:T(8,128)S(1)}, f32[3,32,128]{2,1,0:T(8,128)S(1)}, f32[3,32,128]{2,1,0:T(8,128)S(1)}) custom-call(f32[4096,128]{1,0:T(8,128)} %bitcast.2, f32[3,32,128]{2,1,0:T(8,128)} %baro_hbm.1, s32[32,128]{1,0:T(8,128)} %lev_hbm.1), custom_call_target="tpu_custom_call" | custom-call | tf_op jit(solution)/shard_map/ocean_step/pallas_call | solution.py:595
  27.2 1.4 %finish.1 = (f32[4096,128]{1,0:T(8,128)}, f32[3,32,128]{2,1,0:T(8,128)}) custom-call(f32[4096,128]{1,0:T(8,128)S(1)} %get-tuple-element.7.star, f32[3,32,128]{2,1,0:T(8,128)S(1)} %get-tuple-element.8.baro, f32[3,32,128]{2,1,0:T(8,128)S(1)} %get-tuple-element.9.shift), custom_call_target="tpu_custom_call" | custom-call | tf_op jit(solution)/shard_map/finish/pallas_call | solution.py:627

commit v3 on v2

--- a/solution.py
+++ b/solution.py
@@ -12,6 +12,7 @@
 TX = 32
 TY = 128
 RIM = 32
+MORE = 8
 F32 = jnp.float32
 
 
@@ -28,6 +29,8 @@
 
 
 def unrolled(n, times, body, carry):
+    times = min(n, times)
+
     def several(o, carry):
         for j in range(times):
             carry = body(o * times + j, carry)
@@ -95,8 +98,14 @@
     col_b_out,
     col_b_in,
     force,
+    force_d,
     frim_out,
     frim_in,
+    eta_ref,
+    u_ref,
+    v_ref,
+    lev_ref,
+    coef,
     local_sem,
     send_sem,
     recv_sem,
@@ -253,7 +262,7 @@
             last_b = jnp.where(lane == lax.rem(f * kk + k + TY - 1, TY), moved, last_b)
         return press, first_a, last_a, first_b, last_b
 
-    _, first_a, last_a, first_b, last_b = unrolled(kk, 2, gather, (zero,) * 5)
+    _, first_a, last_a, first_b, last_b = unrolled(kk, MORE, gather, (zero,) * 5)
     last_a = turn(last_a, 1, 1)
     last_b = turn(last_b, 1, 1)
     first_lev = jnp.broadcast_to(lev[:, 0:1], (TX, TY))
@@ -265,6 +274,10 @@
     col_b_out[1] = last_b
     for side, x in ((0, 0), (1, TX - 1)):
         row_a_out[side, pl.ds(2 * kk, kk), :] = press_ref[pl.ds(x, kk, stride=TX), :]
+
+    pl.semaphore_wait(barrier, greeted)
+    for x in links_a + links_rim + links_2d + links_b:
+        x.start()
 
     face_e = jnp.where(row == TX - 1, 0.0, jnp.minimum(lev, turn(lev, -1, 0)))
     face_n = jnp.where(lane == TY - 1, 0.0, jnp.minimum(lev, turn(lev, -1, 1)))
@@ -316,13 +329,8 @@
             out_ref[at_level(f * kk + k), :] = jnp.where(wet, new, 0.0)
         return carry
 
-    sum_u, sum_v, col_u, col_v = unrolled(kk, 2, momentum, (zero,) * 4)
-
-    pl.semaphore_wait(barrier, greeted)
-    for x in links_a + links_rim + links_2d + links_b:
-        x.start()
-
-    unrolled(kk, 2, tracers, 0)
+    sum_u, sum_v, col_u, col_v = unrolled(kk, 4, momentum, (zero,) * 4)
+    unrolled(kk, MORE, tracers, 0)
 
     for x in links_a:
         x.wait_recv()
@@ -368,8 +376,8 @@
     extra_v += jnp.where(row == 0, total(rows_add[1][2]), 0.0)
     extra_v += jnp.where(lane == TY - 1, across(cols_add[0][1], in_vp), 0.0)
     extra_v += jnp.where(lane == 0, across(cols_add[1][1], in_vp), 0.0)
-    force_u = (sum_u + extra_u) * inverse
-    force_v = (sum_v + extra_v) * inverse
+    force_u = (sum_u + extra_u) * (0.3 * inverse)
+    force_v = (sum_v + extra_v) * (0.3 * inverse)
     force[0, own, :] = force_u
     force[1, own, :] = force_v
     half = TX // 2
@@ -421,135 +429,124 @@
     mixed = [jnp.where(odd, north, south), jnp.where(odd, south, north)]
     outer = jnp.logical_or(lane == 0, lane == TY - 1)
 
-    def patch_columns(o, carry):
-        for j in range(4):
-            i = o * 4 + j
-            add = pltpu.roll(mixed[j % 2], lax.rem(TY - i, TY), 1)
-            out_ref[at_level(i), :] = out_ref[at_level(i), :] + jnp.where(outer, add, 0.0)
+    def patch_columns(i, carry):
+        for j in range(2):
+            add = pltpu.roll(mixed[j], lax.rem(TY - (2 * i + j), TY), 1)
+            at = at_level(2 * i + j)
+            out_ref[at, :] = out_ref[at, :] + jnp.where(outer, add, 0.0)
         return carry
 
-    lax.fori_loop(0, kk, patch_columns, 0)
+    unrolled(2 * kk, 16, patch_columns, 0)
 
     for x in links_2d + links_relay:
         x.wait_recv()
-    state_d = [
-        jnp.concatenate([unpack(rim_in[j], rim_in[3 + j], f, lane) for j in range(3)], axis=0)
-        for f in range(4)
-    ]
+
+    def beside(pair, shift):
+        c, d = [turn(x, shift, 1) for x in pair]
+        edge = iota(c.shape, 1) == (TY - 1 if shift < 0 else 0)
+        return jnp.where(edge, d, c), jnp.where(edge, c, d)
+
     wide = 3 * TX
-    lane_w = iota((wide, TY), 1)
-    state = [(flat2d[f], state_d[f]) for f in range(4)]
-    wet = [(a > 0.0).astype(F32) for a in state[3]]
-    depth = [a * (1.0 / kk) for a in state[3]]
-
-    def east(a):
-        return [turn(x, -1, 0) for x in a]
-
-    def west(a):
-        return [turn(x, 1, 0) for x in a]
-
-    def meridional(a, shift, at):
-        c, d = [turn(x, shift, 1) for x in a]
-        edge = iota(c.shape, 1) == at
-        return [jnp.where(edge, d, c), jnp.where(edge, c, d)]
-
-    def north_of(a):
-        return meridional(a, -1, TY - 1)
-
-    def south_of(a):
-        return meridional(a, 1, 0)
-
-    def both(fn, *args):
-        return [fn(*pair) for pair in zip(*args)]
-
-    def times(a, b):
-        return a * b
-
-    coef_e = both(lambda a, b: 0.15 * a * b, wet, east(wet))
-    coef_n = both(lambda a, b: 0.15 * a * b, wet, north_of(wet))
-    y_d = lax.rem(gy * TY + lane_w + jnp.where(lane_w < TY // 2, TY, -TY) + ny * TY, ny * TY)
+    edges = jnp.zeros((2, 8, TY), F32)
+    for ref in (eta_ref, u_ref, v_ref, lev_ref):
+        ref[:, pl.ds(0, 8), :] = edges
+        ref[:, pl.ds(8 + wide, 8), :] = edges
+    lev_ref[0, pl.ds(8, wide), :] = flat2d[3]
+    for j in range(3):
+        part = pl.ds(8 + j * TX, TX)
+        wet_d = None
+        for f, ref in ((3, lev_ref), (0, eta_ref), (1, u_ref), (2, v_ref)):
+            q = unpack(rim_in[j], rim_in[3 + j], f, lane)
+            if f == 3:
+                wet_d = q > 0.0
+                wet_c = flat2d[3, pl.ds(j * TX, TX), :] > 0.0
+                ref[1, part, :] = q
+            else:
+                ref[0, part, :] = jnp.where(wet_c, flat2d[f, pl.ds(j * TX, TX), :], 0.0)
+                ref[1, part, :] = jnp.where(wet_d, q, 0.0)
+    for b in range(0, wide, 8):
+        at, ahead, behind = [pl.ds(8 + b + d, 8) for d in (0, 1, -1)]
+        here = [lev_ref[h, at, :] for h in range(2)]
+        norths = beside(here, -1)
+        souths = beside(here, 1)
+        for h in range(2):
+            is_wet = here[h] > 0.0
+            others = (lev_ref[h, ahead, :], lev_ref[h, behind, :], norths[h], souths[h])
+            faces = [
+                jnp.where(jnp.logical_and(is_wet, other > 0.0), 0.15, 0.0) for other in others
+            ]
+            scale = 1.0 / kk
+            planes = [face * (other * scale) for face, other in zip(faces, others)]
+            planes.append((faces[0] - faces[1]) * (here[h] * scale))
+            planes.append((faces[2] - faces[3]) * (here[h] * scale))
+            for n, plane in enumerate(planes + faces):
+                coef[n, h, pl.ds(b, 8), :] = plane
+
+    lane_8 = iota((8, TY), 1)
+    y_d = lax.rem(gy * TY + lane_8 + jnp.where(lane_8 < TY // 2, TY, -TY) + ny * TY, ny * TY)
     cor = [
-        0.15 * (2.0 * ((gy * TY + lane_w).astype(F32) + 0.5) / row_total - 1.0),
+        0.15 * (2.0 * ((gy * TY + lane_8).astype(F32) + 0.5) / row_total - 1.0),
         0.15 * (2.0 * (y_d.astype(F32) + 0.5) / row_total - 1.0),
     ]
-    eta = both(times, wet, state[0])
-    vel_u = both(times, wet, state[1])
-    vel_v = both(times, wet, state[2])
 
     for x in links_force:
         x.wait_recv()
-    force_d = [
-        jnp.concatenate(
-            [
-                unpack(frim_in[j], frim_in[3 + j], 2 * f + h, lane_h)
-                for j in range(3)
-                for h in (0, 1)
-            ],
-            axis=0,
+    for j in range(3):
+        for f in range(2):
+            for h in (0, 1):
+                part = pl.ds(j * TX + h * half, half)
+                force_d[f, part, :] = unpack(frim_in[j], frim_in[3 + j], 2 * f + h, lane_h)
+    push = ((force.at[0], force_d.at[0]), (force.at[1], force_d.at[1]))
+
+    def substep(group, last, totals):
+        low, high = 8 * group, wide - 8 * group
+        for b in range(low, high, 8):
+            at, ahead, behind = [pl.ds(8 + b + d, 8) for d in (0, 1, -1)]
+            c_at = pl.ds(b, 8)
+            v = [v_ref[h, at, :] for h in range(2)]
+            vn = beside(v, -1)
+            vs = beside(v, 1)
+            for h in range(2):
+                c = [coef[n, h, c_at, :] for n in range(6)]
+                x = (c[0] * u_ref[h, ahead, :] - c[1] * u_ref[h, behind, :]) + c[4] * u_ref[h, at, :]
+                y = (c[2] * vn[h] - c[3] * vs[h]) + c[5] * v[h]
+                eta_ref[h, at, :] = eta_ref[h, at, :] - (x + y)
+        if last:
+            low, high = low + 8, high - 8
+        total_u, total_v = [], []
+        for b in range(low, high, 8):
+            at, ahead, behind = [pl.ds(8 + b + d, 8) for d in (0, 1, -1)]
+            c_at = pl.ds(b, 8)
+            e = [eta_ref[h, at, :] for h in range(2)]
+            en = beside(e, -1)
+            es = beside(e, 1)
+            for h in range(2):
+                c = [coef[n, h, c_at, :] for n in range(6, 10)]
+                gx_eta = c[0] * (eta_ref[h, ahead, :] - e[h]) + c[1] * (e[h] - eta_ref[h, behind, :])
+                gy_eta = c[2] * (en[h] - e[h]) + c[3] * (e[h] - es[h])
+                u = u_ref[h, at, :]
+                v = v_ref[h, at, :]
+                new_u = (u - gx_eta) + (cor[h] * v + push[0][h][c_at, :])
+                new_v = (v - gy_eta) - (cor[h] * u - push[1][h][c_at, :])
+                u_ref[h, at, :] = new_u
+                v_ref[h, at, :] = new_v
+                if h == 0 and TX <= b < 2 * TX:
+                    total_u.append(new_u)
+                    total_v.append(new_v)
+        return (
+            totals[0] + jnp.concatenate(total_u, axis=0),
+            totals[1] + jnp.concatenate(total_v, axis=0),
         )
-        for f in range(2)
-    ]
-    push_u = both(lambda w, a: 0.3 * w * a, wet, (force[0], force_d[0]))
-    push_v = both(lambda w, a: 0.3 * w * a, wet, (force[1], force_d[1]))
-    total_u = zero
-    total_v = zero
-
+
+    totals = (zero, zero)
     per = NSUB // 4
     for group in range(4):
-        if group:
-
-            def cut(pair):
-                return [a[8 : a.shape[0] - 8] for a in pair]
-
-            eta, vel_u, vel_v, push_u, push_v, coef_e, coef_n, cor, depth = [
-                cut(a) for a in (eta, vel_u, vel_v, push_u, push_v, coef_e, coef_n, cor, depth)
-            ]
-        here = TX - 8 * group
-
-        def substep(_, carry):
-            eta, vel_u, vel_v, total_u, total_v = carry
-            flow_u = both(times, depth, vel_u)
-            flow_v = both(times, depth, vel_v)
-            flux_e = both(lambda c, a, b: c * (a + b), coef_e, flow_u, east(flow_u))
-            flux_n = both(lambda c, a, b: c * (a + b), coef_n, flow_v, north_of(flow_v))
-            eta = both(
-                lambda h, e, w, n, s: h - ((e - w) + (n - s)),
-                eta,
-                flux_e,
-                west(flux_e),
-                flux_n,
-                south_of(flux_n),
-            )
-            grad_e = both(lambda c, a, b: c * (b - a), coef_e, eta, east(eta))
-            grad_n = both(lambda c, a, b: c * (b - a), coef_n, eta, north_of(eta))
-            new_u = both(
-                lambda u, v, f, p, a, b: (u - (a + b)) + (f * v + p),
-                vel_u,
-                vel_v,
-                cor,
-                push_u,
-                grad_e,
-                west(grad_e),
-            )
-            new_v = both(
-                lambda v, u, f, p, a, b: (v - (a + b)) - (f * u - p),
-                vel_v,
-                vel_u,
-                cor,
-                push_v,
-                grad_n,
-                south_of(grad_n),
-            )
-            total_u = total_u + new_u[0][here : here + TX]
-            total_v = total_v + new_v[0][here : here + TX]
-            return eta, new_u, new_v, total_u, total_v
-
-        eta, vel_u, vel_v, total_u, total_v = lax.fori_loop(
-            0, per, substep, (eta, vel_u, vel_v, total_u, total_v)
-        )
-
-    for f, a in enumerate((eta, vel_u, vel_v)):
-        baro_out[f] = a[0][8 : 8 + TX]
+        for i in range(per):
+            totals = substep(group, i == per - 1, totals)
+    total_u, total_v = totals
+
+    for f, ref in enumerate((eta_ref, u_ref, v_ref)):
+        baro_out[f] = ref[0, pl.ds(8 + TX, TX), :]
     shift_out[0] = total_u * (1.0 / NSUB) - mean_u
     shift_out[1] = total_v * (1.0 / NSUB) - mean_v
     shift_out[2] = lev
@@ -613,8 +610,14 @@
             pltpu.VMEM((2, TX, TY), F32),
             pltpu.VMEM((2, TX, TY), F32),
             pltpu.VMEM((2, 3 * TX, TY), F32),
+            pltpu.VMEM((2, 3 * TX, TY), F32),
             pltpu.VMEM((2, TX // 2, TY), F32),
             pltpu.VMEM((6, TX // 2, TY), F32),
+            pltpu.VMEM((2, 3 * TX + 16, TY), F32),
+            pltpu.VMEM((2, 3 * TX + 16, TY), F32),
+            pltpu.VMEM((2, 3 * TX + 16, TY), F32),
+            pltpu.VMEM((2, 3 * TX + 16, TY), F32),
+            pltpu.VMEM((10, 2, 3 * TX, TY), F32),
             pltpu.SemaphoreType.DMA((3,)),
             pltpu.SemaphoreType.DMA((links,)),
             pltpu.SemaphoreType.DMA((links,)),

time: 28.8 us -> 22.2 us (0.77)
  Pallas kernels: 28 us -> 21.2 us
    pallas_call x1, Pallas kernels: 26.6 us -> 19.8 us  [per_device(): pl.pallas_call(functools.partial(kernel, kk), out_shape=tuple((pltpu.VMEM...]
where the time goes in v3:
time: 22.2 us; the launch traced here: 21.8 us
  Pallas kernels  21.2 us (95%)
  between operations  0.64 us (3%)
    pallas_call x1, Pallas kernels, per_device(): pl.pallas_call(functools.partial(kernel, kk), out_shape=tuple((pltpu.VMEM...  19.8 us
    pallas_call x1, Pallas kernels, per_device(): pl.pallas_call(functools.partial(finish, kk), out_shape=(shape(rows, TY),...  1.37 us

profile of v3, /device:TPU:1, one launch (start us, length us, event | category | flops | bytes accessed | tf_op | source)
XLA Modules:
  0.0 21.8 jit_solution(18154804180932232574)
XLA Ops:
  0.6 19.8 %ocean_step.1 = (f32[4096,128]{1,0:T(8,128)S(1)}, f32[3,32,128]{2,1,0:T(8,128)S(1)}, f32[3,32,128]{2,1,0:T(8,128)S(1)}) custom-call(f32[4096,128]{1,0:T(8,128)} %bitcast.2, f32[3,32,128]{2,1,0:T(8,128)} %baro_hbm.1, s32[32,128]{1,0:T(8,128)} %lev_hbm.1), custom_call_target="tpu_custom_call" | custom-call | tf_op jit(solution)/shard_map/ocean_step/pallas_call | solution.py:592
  20.5 1.4 %finish.1 = (f32[4096,128]{1,0:T(8,128)}, f32[3,32,128]{2,1,0:T(8,128)}) custom-call(f32[4096,128]{1,0:T(8,128)S(1)} %get-tuple-element.7.star, f32[3,32,128]{2,1,0:T(8,128)S(1)} %get-tuple-element.8.baro, f32[3,32,128]{2,1,0:T(8,128)S(1)} %get-tuple-element.9.shift), custom_call_target="tpu_custom_call" | custom-call | tf_op jit(solution)/shard_map/finish/pallas_call | solution.py:630

commit v4 on v3

--- a/solution.py
+++ b/solution.py
@@ -107,6 +107,7 @@
     lev_ref,
     coef,
     local_sem,
+    load_sem,
     send_sem,
     recv_sem,
 ):
@@ -128,24 +129,29 @@
 
     @pl.when(has_n)
     def _():
-        for x in (xw, xe, gx):
-            greet(x, yn)
+        greet(gx, yn)
 
     @pl.when(has_s)
     def _():
-        for x in (xw, xe, gx):
-            greet(x, ys)
+        greet(gx, ys)
 
     greet(xw, gy)
     greet(xe, gy)
-    greeted = 2 + 3 * (has_n.astype(jnp.int32) + has_s.astype(jnp.int32))
-
-    load_o = pltpu.make_async_copy(ocean_hbm, oc, local_sem.at[0])
+    greeted = 2 + has_n.astype(jnp.int32) + has_s.astype(jnp.int32)
+
+    some = min(kk, MORE)
+
+    def load(c, f):
+        part = pl.ds(pl.multiple_of((f * kk + c * some) * TX, TX), some * TX)
+        return pltpu.make_async_copy(ocean_hbm.at[part, :], oc.at[part, :], load_sem.at[c * 4 + f])
+
     load_b = pltpu.make_async_copy(baro_hbm, flat2d.at[pl.ds(0, 3), pl.ds(TX, TX), :], local_sem.at[1])
     load_l = pltpu.make_async_copy(lev_hbm, lev_i, local_sem.at[2])
     load_l.start()
     load_b.start()
-    load_o.start()
+    for c in range(kk // some):
+        for f in range(4):
+            load(c, f).start()
 
     lane = iota((TX, TY), 1)
     row = iota((TX, TY), 0)
@@ -237,12 +243,6 @@
     north, south = pack([flat2d[f, own, :] for f in range(4)], lane)
     rim_out[0] = north
     rim_out[1] = south
-
-    load_o.wait()
-    for side, x in ((0, 0), (1, TX - 1)):
-        row_a_out[side, pl.ds(0, 2 * kk), :] = oc[pl.ds(x, 2 * kk, stride=TX), :]
-        row_b_out[side] = oc[pl.ds(2 * kk * TX + x, 2 * kk, stride=TX), :]
-        row_a_out[side, pl.ds(3 * kk, 8), :] = jnp.broadcast_to(lev[x : x + 1], (8, TY))
 
     def gather(k, carry):
         press, first_a, last_a, first_b, last_b = carry
@@ -262,7 +262,14 @@
             last_b = jnp.where(lane == lax.rem(f * kk + k + TY - 1, TY), moved, last_b)
         return press, first_a, last_a, first_b, last_b
 
-    _, first_a, last_a, first_b, last_b = unrolled(kk, MORE, gather, (zero,) * 5)
+    def gather_chunk(c, carry):
+        for f in range(4):
+            load(c, f).wait()
+        for j in range(some):
+            carry = gather(c * some + j, carry)
+        return carry
+
+    _, first_a, last_a, first_b, last_b = lax.fori_loop(0, kk // some, gather_chunk, (zero,) * 5)
     last_a = turn(last_a, 1, 1)
     last_b = turn(last_b, 1, 1)
     first_lev = jnp.broadcast_to(lev[:, 0:1], (TX, TY))
@@ -273,7 +280,10 @@
     col_b_out[0] = first_b
     col_b_out[1] = last_b
     for side, x in ((0, 0), (1, TX - 1)):
+        row_a_out[side, pl.ds(0, 2 * kk), :] = oc[pl.ds(x, 2 * kk, stride=TX), :]
         row_a_out[side, pl.ds(2 * kk, kk), :] = press_ref[pl.ds(x, kk, stride=TX), :]
+        row_a_out[side, pl.ds(3 * kk, 8), :] = jnp.broadcast_to(lev[x : x + 1], (8, TY))
+        row_b_out[side] = oc[pl.ds(2 * kk * TX + x, 2 * kk, stride=TX), :]
 
     pl.semaphore_wait(barrier, greeted)
     for x in links_a + links_rim + links_2d + links_b:
@@ -489,17 +499,9 @@
         0.15 * (2.0 * (y_d.astype(F32) + 0.5) / row_total - 1.0),
     ]
 
-    for x in links_force:
-        x.wait_recv()
-    for j in range(3):
-        for f in range(2):
-            for h in (0, 1):
-                part = pl.ds(j * TX + h * half, half)
-                force_d[f, part, :] = unpack(frim_in[j], frim_in[3 + j], 2 * f + h, lane_h)
     push = ((force.at[0], force_d.at[0]), (force.at[1], force_d.at[1]))
 
-    def substep(group, last, totals):
-        low, high = 8 * group, wide - 8 * group
+    def update_eta(low, high):
         for b in range(low, high, 8):
             at, ahead, behind = [pl.ds(8 + b + d, 8) for d in (0, 1, -1)]
             c_at = pl.ds(b, 8)
@@ -511,8 +513,8 @@
                 x = (c[0] * u_ref[h, ahead, :] - c[1] * u_ref[h, behind, :]) + c[4] * u_ref[h, at, :]
                 y = (c[2] * vn[h] - c[3] * vs[h]) + c[5] * v[h]
                 eta_ref[h, at, :] = eta_ref[h, at, :] - (x + y)
-        if last:
-            low, high = low + 8, high - 8
+
+    def update_velocity(low, high, pushed, halves, totals):
         total_u, total_v = [], []
         for b in range(low, high, 8):
             at, ahead, behind = [pl.ds(8 + b + d, 8) for d in (0, 1, -1)]
@@ -520,29 +522,54 @@
             e = [eta_ref[h, at, :] for h in range(2)]
             en = beside(e, -1)
             es = beside(e, 1)
-            for h in range(2):
+            for h in range(halves):
                 c = [coef[n, h, c_at, :] for n in range(6, 10)]
                 gx_eta = c[0] * (eta_ref[h, ahead, :] - e[h]) + c[1] * (e[h] - eta_ref[h, behind, :])
                 gy_eta = c[2] * (en[h] - e[h]) + c[3] * (e[h] - es[h])
                 u = u_ref[h, at, :]
                 v = v_ref[h, at, :]
-                new_u = (u - gx_eta) + (cor[h] * v + push[0][h][c_at, :])
-                new_v = (v - gy_eta) - (cor[h] * u - push[1][h][c_at, :])
+                add_u = cor[h] * v
+                add_v = cor[h] * u
+                if pushed:
+                    add_u = add_u + push[0][h][c_at, :]
+                    add_v = add_v - push[1][h][c_at, :]
+                new_u = (u - gx_eta) + add_u
+                new_v = (v - gy_eta) - add_v
                 u_ref[h, at, :] = new_u
                 v_ref[h, at, :] = new_v
                 if h == 0 and TX <= b < 2 * TX:
                     total_u.append(new_u)
                     total_v.append(new_v)
+        if not pushed:
+            return None
         return (
             totals[0] + jnp.concatenate(total_u, axis=0),
             totals[1] + jnp.concatenate(total_v, axis=0),
         )
 
-    totals = (zero, zero)
+    update_eta(0, wide)
+    update_velocity(0, wide, False, 2, None)
+    for x in links_force:
+        x.wait_recv()
+    for j in range(3):
+        for f, ref in ((0, u_ref), (1, v_ref)):
+            for h in (0, 1):
+                at = j * TX + h * half
+                part = pl.ds(at, half)
+                inner = pl.ds(8 + at, half)
+                add = unpack(frim_in[j], frim_in[3 + j], 2 * f + h, lane_h)
+                force_d[f, part, :] = add
+                ref[1, inner, :] = ref[1, inner, :] + add
+                ref[0, inner, :] = ref[0, inner, :] + force[f, part, :]
+    totals = (u_ref[0, pl.ds(8 + TX, TX), :], v_ref[0, pl.ds(8 + TX, TX), :])
     per = NSUB // 4
-    for group in range(4):
-        for i in range(per):
-            totals = substep(group, i == per - 1, totals)
+    for step in range(1, NSUB):
+        group, i = step // per, step % per
+        low, high = 8 * group, wide - 8 * group
+        update_eta(low, high)
+        if i == per - 1:
+            low, high = low + 8, high - 8
+        totals = update_velocity(low, high, True, 1 if step == NSUB - 1 else 2, totals)
     total_u, total_v = totals
 
     for f, ref in enumerate((eta_ref, u_ref, v_ref)):
@@ -619,6 +646,7 @@
             pltpu.VMEM((2, 3 * TX + 16, TY), F32),
             pltpu.VMEM((10, 2, 3 * TX, TY), F32),
             pltpu.SemaphoreType.DMA((3,)),
+            pltpu.SemaphoreType.DMA((4 * max(1, kk // MORE),)),
             pltpu.SemaphoreType.DMA((links,)),
             pltpu.SemaphoreType.DMA((links,)),
         ],

time: 22.2 us -> 22.4 us (level); the launches traced: 21.8 us -> 22.3 us
  Pallas kernels: 21.2 us -> 21.7 us
    pallas_call x1, Pallas kernels: 19.8 us -> 20.3 us  [per_device(): pl.pallas_call(functools.partial(kernel, kk), out_shape=tuple((pltpu.VMEM...]
where the time goes in v4:
time: 22.4 us; the launch traced here: 22.3 us
  Pallas kernels  21.7 us (97%)
  between operations  0.64 us (3%)
    pallas_call x1, Pallas kernels, per_device(): pl.pallas_call(functools.partial(kernel, kk), out_shape=tuple((pltpu.VMEM...  20.3 us
    pallas_call x1, Pallas kernels, per_device(): pl.pallas_call(functools.partial(finish, kk), out_shape=(shape(rows, TY),...  1.37 us

profile of v4, /device:TPU:1, one launch (start us, length us, event | category | flops | bytes accessed | tf_op | source)
XLA Modules:
  0.0 22.3 jit_solution(3253183905873124820)
XLA Ops:
  0.6 20.3 %ocean_step.1 = (f32[4096,128]{1,0:T(8,128)S(1)}, f32[3,32,128]{2,1,0:T(8,128)S(1)}, f32[3,32,128]{2,1,0:T(8,128)S(1)}) custom-call(f32[4096,128]{1,0:T(8,128)} %bitcast.2, f32[3,32,128]{2,1,0:T(8,128)} %baro_hbm.1, s32[32,128]{1,0:T(8,128)} %lev_hbm.1), custom_call_target="tpu_custom_call" | custom-call | tf_op jit(solution)/shard_map/ocean_step/pallas_call | solution.py:619
  20.9 1.4 %finish.1 = (f32[4096,128]{1,0:T(8,128)}, f32[3,32,128]{2,1,0:T(8,128)}) custom-call(f32[4096,128]{1,0:T(8,128)S(1)} %get-tuple-element.7.star, f32[3,32,128]{2,1,0:T(8,128)S(1)} %get-tuple-element.8.baro, f32[3,32,128]{2,1,0:T(8,128)S(1)} %get-tuple-element.9.shift), custom_call_target="tpu_custom_call" | custom-call | tf_op jit(solution)/shard_map/finish/pallas_call | solution.py:658

commit v5 on v4

--- a/solution.py
+++ b/solution.py
@@ -93,12 +93,11 @@
     row_a_in,
     row_b_out,
     row_b_in,
-    col_a_out,
-    col_a_in,
+    cols_in,
     col_b_out,
     col_b_in,
     force,
-    force_d,
+    push,
     frim_out,
     frim_in,
     eta_ref,
@@ -190,8 +189,6 @@
     after = pl.ds(2 * TX, TX)
     before = pl.ds(0, TX)
     links_a = [
-        southward(col_a_out.at[0], col_a_in.at[0]),
-        northward(col_a_out.at[1], col_a_in.at[1]),
         westward(row_a_out.at[0], row_a_in.at[0]),
         eastward(row_a_out.at[1], row_a_in.at[1]),
     ]
@@ -199,7 +196,10 @@
         southward(rim_out.at[1], rim_in.at[1]),
         northward(rim_out.at[0], rim_in.at[4]),
     ]
+    columns = rim_out.at[:, pl.ds(TX, TX), :]
     links_2d = [
+        westward(columns, cols_in.at[1]),
+        eastward(columns, cols_in.at[0]),
         westward(flat2d.at[:, own, :], flat2d.at[:, after, :]),
         eastward(flat2d.at[:, own, :], flat2d.at[:, before, :]),
     ]
@@ -228,12 +228,12 @@
 
     @pl.when(jnp.logical_not(has_n))
     def _():
-        rim_in[0:3] = jnp.zeros((3, TX, TY), F32)
+        rim_in[0:3] = jnp.zeros((3, 2 * TX, TY), F32)
         frim_in[0:3] = jnp.zeros((3, TX // 2, TY), F32)
 
     @pl.when(jnp.logical_not(has_s))
     def _():
-        rim_in[3:6] = jnp.zeros((3, TX, TY), F32)
+        rim_in[3:6] = jnp.zeros((3, 2 * TX, TY), F32)
         frim_in[3:6] = jnp.zeros((3, TX // 2, TY), F32)
 
     load_l.wait()
@@ -241,8 +241,8 @@
     flat2d[3, own, :] = lev
     load_b.wait()
     north, south = pack([flat2d[f, own, :] for f in range(4)], lane)
-    rim_out[0] = north
-    rim_out[1] = south
+    rim_out[0, pl.ds(0, TX), :] = north
+    rim_out[1, pl.ds(0, TX), :] = south
 
     def gather(k, carry):
         press, first_a, last_a, first_b, last_b = carry
@@ -275,8 +275,8 @@
     first_lev = jnp.broadcast_to(lev[:, 0:1], (TX, TY))
     last_lev = jnp.broadcast_to(lev[:, TY - 1 : TY], (TX, TY))
     in_lev = lane >= 96
-    col_a_out[0] = jnp.where(in_lev, first_lev, first_a)
-    col_a_out[1] = jnp.where(in_lev, last_lev, last_a)
+    rim_out[0, pl.ds(TX, TX), :] = jnp.where(in_lev, last_lev, last_a)
+    rim_out[1, pl.ds(TX, TX), :] = jnp.where(in_lev, first_lev, first_a)
     col_b_out[0] = first_b
     col_b_out[1] = last_b
     for side, x in ((0, 0), (1, TX - 1)):
@@ -356,38 +356,16 @@
             for f in range(3)
         ]
         rows_add.append((wet, ju - (0.5 * sign) * jp, jv))
-    cols_add = []
-    level_l = jnp.where(lane < kk, lane, jnp.where(lane < 2 * kk, lane - kk, lane - 2 * kk)).astype(F32)
-    in_u = lane < kk
-    in_v = jnp.logical_and(lane >= kk, lane < 2 * kk)
-    in_p = jnp.logical_and(lane >= 2 * kk, lane < 3 * kk)
-    for side, sign in ((0, 1.0), (1, -1.0)):
-        mine = col_a_out[1 - side]
-        theirs = col_a_in[side]
-        their_lev = jnp.broadcast_to(theirs[:, TY - 1 : TY], (TX, TY))
-        my_lev = last_lev if side == 0 else first_lev
-        wet = jnp.logical_and(level_l < jnp.minimum(my_lev, their_lev), (has_n, has_s)[side])
-        jump = jnp.where(wet, theirs - mine, 0.0)
-        both = jnp.where(in_p, (-0.5 * sign) * jump, jump)
-        cols_add.append((wet, both))
 
     def total(a):
         return jnp.sum(a, axis=0, keepdims=True)
 
-    def across(a, mask):
-        return jnp.sum(jnp.where(mask, a, 0.0), axis=1, keepdims=True)
-
-    in_vp = jnp.logical_or(in_v, in_p)
-    extra_u = jnp.where(row == TX - 1, total(rows_add[0][1]), 0.0)
-    extra_u += jnp.where(row == 0, total(rows_add[1][1]), 0.0)
-    extra_u += jnp.where(lane == TY - 1, across(cols_add[0][1], in_u), 0.0)
-    extra_u += jnp.where(lane == 0, across(cols_add[1][1], in_u), 0.0)
-    extra_v = jnp.where(row == TX - 1, total(rows_add[0][2]), 0.0)
-    extra_v += jnp.where(row == 0, total(rows_add[1][2]), 0.0)
-    extra_v += jnp.where(lane == TY - 1, across(cols_add[0][1], in_vp), 0.0)
-    extra_v += jnp.where(lane == 0, across(cols_add[1][1], in_vp), 0.0)
-    force_u = (sum_u + extra_u) * (0.3 * inverse)
-    force_v = (sum_v + extra_v) * (0.3 * inverse)
+    zonal_u = jnp.where(row == TX - 1, total(rows_add[0][1]), 0.0)
+    zonal_u += jnp.where(row == 0, total(rows_add[1][1]), 0.0)
+    zonal_v = jnp.where(row == TX - 1, total(rows_add[0][2]), 0.0)
+    zonal_v += jnp.where(row == 0, total(rows_add[1][2]), 0.0)
+    force_u = (sum_u + zonal_u) * (0.3 * inverse)
+    force_v = (sum_v + zonal_v) * (0.3 * inverse)
     force[0, own, :] = force_u
     force[1, own, :] = force_v
     half = TX // 2
@@ -404,8 +382,43 @@
         x.wait_recv()
     for x in links_relay:
         x.start()
-    mean_u = (col_u + 0.1 * extra_u) * inverse
-    mean_v = (col_v + 0.1 * extra_v) * inverse
+
+    level_l = jnp.where(lane < kk, lane, jnp.where(lane < 2 * kk, lane - kk, lane - 2 * kk)).astype(F32)
+    in_u = lane < kk
+    in_v = jnp.logical_and(lane >= kk, lane < 2 * kk)
+    in_p = jnp.logical_and(lane >= 2 * kk, lane < 3 * kk)
+
+    def across(a, mask):
+        return jnp.sum(jnp.where(mask, a, 0.0), axis=1, keepdims=True)
+
+    def meridional_face(side, mine, theirs):
+        sign = (1.0, -1.0)[side]
+        near, far = (TY - 1, 0) if side == 0 else (0, TY - 1)
+        my_lev, their_lev = [jnp.broadcast_to(a[:, TY - 1 : TY], (TX, TY)) for a in (mine, theirs)]
+        wet = level_l < jnp.minimum(my_lev, their_lev)
+        jump = jnp.where(wet, theirs - mine, 0.0)
+        jump_u = across(jump, in_u)
+        jump_v = across(jump, in_v)
+        jump_p = (0.5 * sign) * across(jump, in_p)
+        here = [jnp.where(lane == near, a, 0.0) for a in (jump_u, jump_v - jump_p)]
+        there = [jnp.where(lane == far, a, 0.0) for a in (-jump_u, -jump_v - jump_p)]
+        scale = [0.3 / jnp.maximum(a, 1.0) for a in (my_lev, their_lev)]
+        return wet, jump, here, [a * scale[0] for a in here], [a * scale[1] for a in there]
+
+    def meridional_faces(j, mine):
+        faces = [
+            meridional_face(side, mine[side], rim_in[3 * side + j, pl.ds(TX, TX), :])
+            for side in range(2)
+        ]
+        for f in range(2):
+            push[f, 0, pl.ds(j * TX, TX), :] = faces[0][3][f] + faces[1][3][f]
+            push[f, 1, pl.ds(j * TX, TX), :] = faces[0][4][f] + faces[1][4][f]
+        return faces
+
+    my_columns = [rim_out[side, pl.ds(TX, TX), :] for side in range(2)]
+    faces = meridional_faces(1, my_columns)
+    mean_u = (col_u + 0.1 * (zonal_u + faces[0][2][0] + faces[1][2][0])) * inverse
+    mean_v = (col_v + 0.1 * (zonal_v + faces[0][2][1] + faces[1][2][1])) * inverse
 
     for x in links_b:
         x.wait_recv()
@@ -422,8 +435,9 @@
             out_ref[at, :] = out_ref[at, :] + weight * jump
     patches = []
     for side, sign in ((0, 1.0), (1, -1.0)):
-        wet, both = cols_add[side]
-        mine = col_a_out[1 - side]
+        wet, jump = faces[side][:2]
+        both = jnp.where(in_p, (-0.5 * sign) * jump, jump)
+        mine = my_columns[side]
         first = 0.1 * (both + jnp.where(in_v, turn(jnp.where(in_p, both, 0.0), -kk, 1), 0.0))
         v = jnp.where(lane < kk, turn(mine, -kk, 1), mine)
         jump = jnp.where(
@@ -466,7 +480,7 @@
         part = pl.ds(8 + j * TX, TX)
         wet_d = None
         for f, ref in ((3, lev_ref), (0, eta_ref), (1, u_ref), (2, v_ref)):
-            q = unpack(rim_in[j], rim_in[3 + j], f, lane)
+            q = unpack(rim_in[j, pl.ds(0, TX), :], rim_in[3 + j, pl.ds(0, TX), :], f, lane)
             if f == 3:
                 wet_d = q > 0.0
                 wet_c = flat2d[3, pl.ds(j * TX, TX), :] > 0.0
@@ -499,7 +513,8 @@
         0.15 * (2.0 * (y_d.astype(F32) + 0.5) / row_total - 1.0),
     ]
 
-    push = ((force.at[0], force_d.at[0]), (force.at[1], force_d.at[1]))
+    meridional_faces(0, [cols_in[0, side] for side in range(2)])
+    meridional_faces(2, [cols_in[1, side] for side in range(2)])
 
     def update_eta(low, high):
         for b in range(low, high, 8):
@@ -531,8 +546,8 @@
                 add_u = cor[h] * v
                 add_v = cor[h] * u
                 if pushed:
-                    add_u = add_u + push[0][h][c_at, :]
-                    add_v = add_v - push[1][h][c_at, :]
+                    add_u = add_u + push[0, h, c_at, :]
+                    add_v = add_v - push[1, h, c_at, :]
                 new_u = (u - gx_eta) + add_u
                 new_v = (v - gy_eta) - add_v
                 u_ref[h, at, :] = new_u
@@ -557,10 +572,11 @@
                 at = j * TX + h * half
                 part = pl.ds(at, half)
                 inner = pl.ds(8 + at, half)
-                add = unpack(frim_in[j], frim_in[3 + j], 2 * f + h, lane_h)
-                force_d[f, part, :] = add
-                ref[1, inner, :] = ref[1, inner, :] + add
-                ref[0, inner, :] = ref[0, inner, :] + force[f, part, :]
+                beyond = unpack(frim_in[j], frim_in[3 + j], 2 * f + h, lane_h)
+                for side, add in ((0, force[f, part, :]), (1, beyond)):
+                    add = push[f, side, part, :] + add
+                    push[f, side, part, :] = add
+                    ref[side, inner, :] = ref[side, inner, :] + add
     totals = (u_ref[0, pl.ds(8 + TX, TX), :], v_ref[0, pl.ds(8 + TX, TX), :])
     per = NSUB // 4
     for step in range(1, NSUB):
@@ -626,18 +642,17 @@
             pltpu.VMEM((kk * TX, TY), F32),
             pltpu.VMEM((TX, TY), jnp.int32),
             pltpu.VMEM((4, 3 * TX, TY), F32),
-            pltpu.VMEM((2, TX, TY), F32),
-            pltpu.VMEM((6, TX, TY), F32),
+            pltpu.VMEM((2, 2 * TX, TY), F32),
+            pltpu.VMEM((6, 2 * TX, TY), F32),
             pltpu.VMEM((2, 3 * kk + 8, TY), F32),
             pltpu.VMEM((2, 3 * kk + 8, TY), F32),
             pltpu.VMEM((2, 2 * kk, TY), F32),
             pltpu.VMEM((2, 2 * kk, TY), F32),
-            pltpu.VMEM((2, TX, TY), F32),
-            pltpu.VMEM((2, TX, TY), F32),
+            pltpu.VMEM((2, 2, TX, TY), F32),
             pltpu.VMEM((2, TX, TY), F32),
             pltpu.VMEM((2, TX, TY), F32),
             pltpu.VMEM((2, 3 * TX, TY), F32),
-            pltpu.VMEM((2, 3 * TX, TY), F32),
+            pltpu.VMEM((2, 2, 3 * TX, TY), F32),
             pltpu.VMEM((2, TX // 2, TY), F32),
             pltpu.VMEM((6, TX // 2, TY), F32),
             pltpu.VMEM((2, 3 * TX + 16, TY), F32),

time: 22.4 us -> 23 us (1.027)
  the two profiles are of different devices: /device:TPU:1 before, /device:TPU:24 now
where the time goes in v5:
time: 23 us; the launch traced here: 22.9 us
  Pallas kernels  22.3 us (97%)
  between operations  0.64 us (3%)
    pallas_call x1, Pallas kernels, per_device(): pl.pallas_call(functools.partial(kernel, kk), out_shape=tuple((pltpu.VMEM...  20.9 us
    pallas_call x1, Pallas kernels, per_device(): pl.pallas_call(functools.partial(finish, kk), out_shape=(shape(rows, TY),...  1.37 us

profile of v5, /device:TPU:24, one launch (start us, length us, event | category | flops | bytes accessed | tf_op | source)
XLA Modules:
  0.0 22.9 jit_solution(11807133614789036856)
XLA Ops:
  0.6 20.9 %ocean_step.1 = (f32[4096,128]{1,0:T(8,128)S(1)}, f32[3,32,128]{2,1,0:T(8,128)S(1)}, f32[3,32,128]{2,1,0:T(8,128)S(1)}) custom-call(f32[4096,128]{1,0:T(8,128)} %bitcast.2, f32[3,32,128]{2,1,0:T(8,128)} %baro_hbm.1, s32[32,128]{1,0:T(8,128)} %lev_hbm.1), custom_call_target="tpu_custom_call" | custom-call | tf_op jit(solution)/shard_map/ocean_step/pallas_call | solution.py:635
  21.6 1.4 %finish.1 = (f32[4096,128]{1,0:T(8,128)}, f32[3,32,128]{2,1,0:T(8,128)}) custom-call(f32[4096,128]{1,0:T(8,128)S(1)} %get-tuple-element.7.star, f32[3,32,128]{2,1,0:T(8,128)S(1)} %get-tuple-element.8.baro, f32[3,32,128]{2,1,0:T(8,128)S(1)} %get-tuple-element.9.shift), custom_call_target="tpu_custom_call" | custom-call | tf_op jit(solution)/shard_map/finish/pallas_call | solution.py:673

commit v6 on v5

--- a/solution.py
+++ b/solution.py
@@ -93,6 +93,8 @@
     row_a_in,
     row_b_out,
     row_b_in,
+    col_a_out,
+    col_a_in,
     cols_in,
     col_b_out,
     col_b_in,
@@ -196,25 +198,37 @@
         southward(rim_out.at[1], rim_in.at[1]),
         northward(rim_out.at[0], rim_in.at[4]),
     ]
-    columns = rim_out.at[:, pl.ds(TX, TX), :]
+    links_col = [
+        southward(col_a_out.at[1], col_a_in.at[1]),
+        northward(col_a_out.at[0], col_a_in.at[4]),
+    ]
+    links_cols = [
+        westward(col_a_out, cols_in.at[1]),
+        eastward(col_a_out, cols_in.at[0]),
+    ]
     links_2d = [
-        westward(columns, cols_in.at[1]),
-        eastward(columns, cols_in.at[0]),
         westward(flat2d.at[:, own, :], flat2d.at[:, after, :]),
         eastward(flat2d.at[:, own, :], flat2d.at[:, before, :]),
     ]
-    links_b = [
+    links_row_b = [
+        westward(row_b_out.at[0], row_b_in.at[0]),
+        eastward(row_b_out.at[1], row_b_in.at[1]),
+    ]
+    links_col_b = [
         southward(col_b_out.at[0], col_b_in.at[0]),
         northward(col_b_out.at[1], col_b_in.at[1]),
-        westward(row_b_out.at[0], row_b_in.at[0]),
-        eastward(row_b_out.at[1], row_b_in.at[1]),
-    ]
-    links_relay = [
-        link(rim_in.at[1], rim_in.at[2], (xw, gy), has_n, has_n),
-        link(rim_in.at[1], rim_in.at[0], (xe, gy), has_n, has_n),
-        link(rim_in.at[4], rim_in.at[5], (xw, gy), has_s, has_s),
-        link(rim_in.at[4], rim_in.at[3], (xe, gy), has_s, has_s),
-    ]
+    ]
+
+    def relay(ref):
+        return [
+            link(ref.at[1], ref.at[2], (xw, gy), has_n, has_n),
+            link(ref.at[1], ref.at[0], (xe, gy), has_n, has_n),
+            link(ref.at[4], ref.at[5], (xw, gy), has_s, has_s),
+            link(ref.at[4], ref.at[3], (xe, gy), has_s, has_s),
+        ]
+
+    links_relay = relay(rim_in)
+    links_col_relay = relay(col_a_in)
     links_force = [
         southward(frim_out.at[1], frim_in.at[0], xe),
         northward(frim_out.at[0], frim_in.at[3], xe),
@@ -228,12 +242,14 @@
 
     @pl.when(jnp.logical_not(has_n))
     def _():
-        rim_in[0:3] = jnp.zeros((3, 2 * TX, TY), F32)
+        rim_in[0:3] = jnp.zeros((3, TX, TY), F32)
+        col_a_in[0:3] = jnp.zeros((3, TX, TY), F32)
         frim_in[0:3] = jnp.zeros((3, TX // 2, TY), F32)
 
     @pl.when(jnp.logical_not(has_s))
     def _():
-        rim_in[3:6] = jnp.zeros((3, 2 * TX, TY), F32)
+        rim_in[3:6] = jnp.zeros((3, TX, TY), F32)
+        col_a_in[3:6] = jnp.zeros((3, TX, TY), F32)
         frim_in[3:6] = jnp.zeros((3, TX // 2, TY), F32)
 
     load_l.wait()
@@ -241,8 +257,29 @@
     flat2d[3, own, :] = lev
     load_b.wait()
     north, south = pack([flat2d[f, own, :] for f in range(4)], lane)
-    rim_out[0, pl.ds(0, TX), :] = north
-    rim_out[1, pl.ds(0, TX), :] = south
+    rim_out[0] = north
+    rim_out[1] = south
+
+    for c in range(kk // some):
+        for f in range(4):
+            load(c, f).wait()
+    level = iota((kk, TY), 0).astype(F32)
+    for side, x in ((0, 0), (1, TX - 1)):
+        row_a_out[side, pl.ds(0, 2 * kk), :] = oc[pl.ds(x, 2 * kk, stride=TX), :]
+        t = oc[pl.ds(2 * kk * TX + x, kk, stride=TX), :]
+        s = oc[pl.ds(3 * kk * TX + x, kk, stride=TX), :]
+        row_b_out[side, pl.ds(0, kk), :] = t
+        row_b_out[side, pl.ds(kk, kk), :] = s
+        row_a_out[side, pl.ds(3 * kk, 8), :] = jnp.broadcast_to(lev[x : x + 1], (8, TY))
+        layers = jnp.where(level < lev[x : x + 1], 0.1 * s - 0.2 * t, 0.0)
+        press = jnp.zeros((1, TY), F32)
+        for k in range(kk):
+            press = press + layers[k : k + 1]
+            row_a_out[side, pl.ds(2 * kk + k, 1), :] = press
+
+    pl.semaphore_wait(barrier, greeted)
+    for x in links_a + links_rim + links_2d + links_row_b:
+        x.start()
 
     def gather(k, carry):
         press, first_a, last_a, first_b, last_b = carry
@@ -263,8 +300,6 @@
         return press, first_a, last_a, first_b, last_b
 
     def gather_chunk(c, carry):
-        for f in range(4):
-            load(c, f).wait()
         for j in range(some):
             carry = gather(c * some + j, carry)
         return carry
@@ -275,18 +310,11 @@
     first_lev = jnp.broadcast_to(lev[:, 0:1], (TX, TY))
     last_lev = jnp.broadcast_to(lev[:, TY - 1 : TY], (TX, TY))
     in_lev = lane >= 96
-    rim_out[0, pl.ds(TX, TX), :] = jnp.where(in_lev, last_lev, last_a)
-    rim_out[1, pl.ds(TX, TX), :] = jnp.where(in_lev, first_lev, first_a)
+    col_a_out[0] = jnp.where(in_lev, last_lev, last_a)
+    col_a_out[1] = jnp.where(in_lev, first_lev, first_a)
     col_b_out[0] = first_b
     col_b_out[1] = last_b
-    for side, x in ((0, 0), (1, TX - 1)):
-        row_a_out[side, pl.ds(0, 2 * kk), :] = oc[pl.ds(x, 2 * kk, stride=TX), :]
-        row_a_out[side, pl.ds(2 * kk, kk), :] = press_ref[pl.ds(x, kk, stride=TX), :]
-        row_a_out[side, pl.ds(3 * kk, 8), :] = jnp.broadcast_to(lev[x : x + 1], (8, TY))
-        row_b_out[side] = oc[pl.ds(2 * kk * TX + x, 2 * kk, stride=TX), :]
-
-    pl.semaphore_wait(barrier, greeted)
-    for x in links_a + links_rim + links_2d + links_b:
+    for x in links_col + links_cols + links_col_b:
         x.start()
 
     face_e = jnp.where(row == TX - 1, 0.0, jnp.minimum(lev, turn(lev, -1, 0)))
@@ -340,11 +368,9 @@
         return carry
 
     sum_u, sum_v, col_u, col_v = unrolled(kk, 4, momentum, (zero,) * 4)
-    unrolled(kk, MORE, tracers, 0)
 
     for x in links_a:
         x.wait_recv()
-    level = iota((kk, TY), 0).astype(F32)
     rows_add = []
     for side, sign in ((0, 1.0), (1, -1.0)):
         mine = row_a_out.at[1 - side]
@@ -382,6 +408,11 @@
         x.wait_recv()
     for x in links_relay:
         x.start()
+    unrolled(kk, MORE, tracers, 0)
+    for x in links_col:
+        x.wait_recv()
+    for x in links_col_relay:
+        x.start()
 
     level_l = jnp.where(lane < kk, lane, jnp.where(lane < 2 * kk, lane - kk, lane - 2 * kk)).astype(F32)
     in_u = lane < kk
@@ -407,7 +438,7 @@
 
     def meridional_faces(j, mine):
         faces = [
-            meridional_face(side, mine[side], rim_in[3 * side + j, pl.ds(TX, TX), :])
+            meridional_face(side, mine[side], col_a_in[3 * side + j])
             for side in range(2)
         ]
         for f in range(2):
@@ -415,12 +446,12 @@
             push[f, 1, pl.ds(j * TX, TX), :] = faces[0][4][f] + faces[1][4][f]
         return faces
 
-    my_columns = [rim_out[side, pl.ds(TX, TX), :] for side in range(2)]
+    my_columns = [col_a_out[side] for side in range(2)]
     faces = meridional_faces(1, my_columns)
     mean_u = (col_u + 0.1 * (zonal_u + faces[0][2][0] + faces[1][2][0])) * inverse
     mean_v = (col_v + 0.1 * (zonal_v + faces[0][2][1] + faces[1][2][1])) * inverse
 
-    for x in links_b:
+    for x in links_row_b + links_col_b:
         x.wait_recv()
     for side, sign, x in ((0, 1.0, TX - 1), (1, -1.0, 0)):
         wet, add_u, add_v = rows_add[side]
@@ -480,7 +511,7 @@
         part = pl.ds(8 + j * TX, TX)
         wet_d = None
         for f, ref in ((3, lev_ref), (0, eta_ref), (1, u_ref), (2, v_ref)):
-            q = unpack(rim_in[j, pl.ds(0, TX), :], rim_in[3 + j, pl.ds(0, TX), :], f, lane)
+            q = unpack(rim_in[j], rim_in[3 + j], f, lane)
             if f == 3:
                 wet_d = q > 0.0
                 wet_c = flat2d[3, pl.ds(j * TX, TX), :] > 0.0
@@ -512,9 +543,6 @@
         0.15 * (2.0 * ((gy * TY + lane_8).astype(F32) + 0.5) / row_total - 1.0),
         0.15 * (2.0 * (y_d.astype(F32) + 0.5) / row_total - 1.0),
     ]
-
-    meridional_faces(0, [cols_in[0, side] for side in range(2)])
-    meridional_faces(2, [cols_in[1, side] for side in range(2)])
 
     def update_eta(low, high):
         for b in range(low, high, 8):
@@ -564,6 +592,10 @@
 
     update_eta(0, wide)
     update_velocity(0, wide, False, 2, None)
+    for x in links_cols + links_col_relay:
+        x.wait_recv()
+    meridional_faces(0, [cols_in[0, side] for side in range(2)])
+    meridional_faces(2, [cols_in[1, side] for side in range(2)])
     for x in links_force:
         x.wait_recv()
     for j in range(3):
@@ -593,7 +625,8 @@
     shift_out[0] = total_u * (1.0 / NSUB) - mean_u
     shift_out[1] = total_v * (1.0 / NSUB) - mean_v
     shift_out[2] = lev
-    for x in links_a + links_rim + links_2d + links_b + links_relay + links_force:
+    every = links_a + links_rim + links_2d + links_row_b + links_col + links_cols + links_col_b
+    for x in every + links_relay + links_col_relay + links_force:
         x.wait_send()
 
 
@@ -627,7 +660,7 @@
     rows = 4 * kk * TX
     hbm = pl.BlockSpec(memory_space=pltpu.HBM)
     vmem = pl.BlockSpec(memory_space=pltpu.VMEM)
-    links = 24
+    links = 32
 
     def shape(*dims):
         return jax.ShapeDtypeStruct(dims, F32)
@@ -642,12 +675,14 @@
             pltpu.VMEM((kk * TX, TY), F32),
             pltpu.VMEM((TX, TY), jnp.int32),
             pltpu.VMEM((4, 3 * TX, TY), F32),
-            pltpu.VMEM((2, 2 * TX, TY), F32),
-            pltpu.VMEM((6, 2 * TX, TY), F32),
+            pltpu.VMEM((2, TX, TY), F32),
+            pltpu.VMEM((6, TX, TY), F32),
             pltpu.VMEM((2, 3 * kk + 8, TY), F32),
             pltpu.VMEM((2, 3 * kk + 8, TY), F32),
             pltpu.VMEM((2, 2 * kk, TY), F32),
             pltpu.VMEM((2, 2 * kk, TY), F32),
+            pltpu.VMEM((2, TX, TY), F32),
+            pltpu.VMEM((6, TX, TY), F32),
             pltpu.VMEM((2, 2, TX, TY), F32),
             pltpu.VMEM((2, TX, TY), F32),
             pltpu.VMEM((2, TX, TY), F32),

time: 23 us -> 22.6 us (0.983)
  the two profiles are of different devices: /device:TPU:24 before, /device:TPU:8 now
where the time goes in v6:
time: 22.6 us; the launch traced here: 22.5 us
  Pallas kernels  21.9 us (97%)
  between operations  0.64 us (3%)
    pallas_call x1, Pallas kernels, per_device(): pl.pallas_call(functools.partial(kernel, kk), out_shape=tuple((pltpu.VMEM...  20.5 us
    pallas_call x1, Pallas kernels, per_device(): pl.pallas_call(functools.partial(finish, kk), out_shape=(shape(rows, TY),...  1.37 us

profile of v6, /device:TPU:8, one launch (start us, length us, event | category | flops | bytes accessed | tf_op | source)
XLA Modules:
  0.0 22.5 jit_solution(4866855784067229306)
XLA Ops:
  0.6 20.5 %ocean_step.1 = (f32[4096,128]{1,0:T(8,128)S(1)}, f32[3,32,128]{2,1,0:T(8,128)S(1)}, f32[3,32,128]{2,1,0:T(8,128)S(1)}) custom-call(f32[4096,128]{1,0:T(8,128)} %bitcast.2, f32[3,32,128]{2,1,0:T(8,128)} %baro_hbm.1, s32[32,128]{1,0:T(8,128)} %lev_hbm.1), custom_call_target="tpu_custom_call" | custom-call | tf_op jit(solution)/shard_map/ocean_step/pallas_call | solution.py:668
  21.1 1.4 %finish.1 = (f32[4096,128]{1,0:T(8,128)}, f32[3,32,128]{2,1,0:T(8,128)}) custom-call(f32[4096,128]{1,0:T(8,128)S(1)} %get-tuple-element.7.star, f32[3,32,128]{2,1,0:T(8,128)S(1)} %get-tuple-element.8.baro, f32[3,32,128]{2,1,0:T(8,128)S(1)} %get-tuple-element.9.shift), custom_call_target="tpu_custom_call" | custom-call | tf_op jit(solution)/shard_map/finish/pallas_call | solution.py:708
